TPU v7x, 32 devices: a whole 2x2x4 slice. The times are simulated.
32 devices in a mesh: win: 2 (over y), row: 4 (over z), col: 4 (over x, core).
Axes of the slice: x: 2, y: 2, z: 4, core: 2. Of those that a mesh axis runs over, the one named last changes fastest.
Arguments:
- records: bfloat16 [32, 4096, 1024], P('win', ('row', 'col'))
- tile_pairs: int32 [4, 4, 4, 2], P('row', 'col'), may hold values from 0 to 3
- tile_count: int32 [4, 4], P('row', 'col'), may hold values from 1 to 4, as said below
- bin_index: int32 [32], replicated, may hold values from 1 to 511, as said below
Outputs:
- cross_tiles: bfloat16 [4, 4, 4, 2, 32, 256, 256], P('row', 'col', 'win')
Inputs may be any that keep to these rules, and one draw needn't show every extreme that they name: Slots 0 to tile_count - 1 of a cell are live; some cell has all 4 live and some cell one. `bin_index`: distinct and increasing; the first is 1 and the last 511.
All inputs are finite; a program needn't handle non-finite values.
Results may differ from a plain program's by a relative error of at most 0.0069.
Values may be sent and summed in bfloat16 or wider, within the bound.
A program may use at most 256 MiB of HBM per device.

v0:
```python
import functools
import math

import jax
import jax.numpy as jnp
from jax import lax
from jax.experimental import pallas as pl
from jax.experimental.pallas import tpu as pltpu
from jax.sharding import PartitionSpec as P

GROUP = 8
UP, DOWN, PARTNER, RIGHT, LEFT, SIBLING = range(6)


def dft_tables(bin_index, length):
    sample_ids = jnp.arange(length, dtype=jnp.int32)
    phases = bin_index[:, None] * sample_ids[None, :] % length
    angles = 2.0 * math.pi / length * phases.astype(jnp.float32)
    window_taper = 0.5 - 0.5 * jnp.cos(2.0 * math.pi / length * sample_ids.astype(jnp.float32))
    cosine = window_taper[None, :] * jnp.cos(angles)
    sine = -window_taper[None, :] * jnp.sin(angles)
    return cosine.astype(jnp.bfloat16), sine.astype(jnp.bfloat16)


def gather_kernel(rows, cols, groups, rec_hbm, cos_ref, sin_ref, sets, rec, spec, own,
                  rec_sem, local_sem, send_sem, recv_sem):
    w, r, q = lax.axis_index("win"), lax.axis_index("row"), lax.axis_index("col")
    chips = cols // 2
    x = q // 2
    other = 1 - w
    sib = q + 1 - 2 * (q % 2)
    mine, theirs = w * groups, other * groups
    device = {
        UP: (w, r + 1, q), DOWN: (w, r - 1, q), PARTNER: (other, r, q),
        RIGHT: (w, r, q + 2), LEFT: (w, r, q - 2), SIBLING: (w, r, sib),
    }
    exists = {
        UP: r < rows - 1, DOWN: r > 0, PARTNER: None,
        RIGHT: x < chips - 1, LEFT: x > 0, SIBLING: None,
    }

    def fetch(i):
        part = pl.ds(i * GROUP, GROUP)
        return pltpu.make_async_copy(rec_hbm.at[part], rec.at[part], rec_sem.at[i])

    for i in range(groups):
        fetch(i).start()

    def guarded(way, f):
        if exists[way] is None:
            f()
        else:
            pl.when(exists[way])(f)

    barrier = pltpu.get_barrier_semaphore()
    for way in range(6):
        guarded(way, lambda way=way: pl.semaphore_signal(
            barrier, inc=1, device_id=device[way], device_id_type=pl.DeviceIdType.MESH))
    ends = sum(exists[way].astype(jnp.int32) for way in (UP, DOWN, RIGHT, LEFT))

    def copy(way, src, slot, g):
        return pltpu.make_async_remote_copy(
            src_ref=src, dst_ref=sets.at[slot, g], send_sem=send_sem.at[way, slot, g],
            recv_sem=recv_sem.at[slot, g], device_id=device[way],
            device_id_type=pl.DeviceIdType.MESH)

    pending = []

    def send(way, src, slot, g, cond=None):
        def go():
            guarded(way, lambda: copy(way, src, slot, g).start())

        def done():
            guarded(way, lambda: copy(way, src, slot, g).wait_send())

        if cond is None:
            go()
        pending.append((cond, done))
        return go

    def arrived(slot, g):
        copy(PARTNER, sets.at[slot, g], slot, g).wait_recv()

    bins = cos_ref.shape[0]
    keeps = []
    for i in range(groups):
        fetch(i).wait()

        def one_window(v, _, i=i):
            table = jnp.concatenate([cos_ref[...], sin_ref[...]], axis=0)
            s = lax.dot_general(table, rec[i * GROUP + v], (((1,), (1,)), ((), ())),
                                preferred_element_type=jnp.float32)
            scale = 1.0 / jnp.sqrt(jnp.mean(s * s, axis=0, keepdims=True) + 1e-06)
            s = s * scale
            for lane in range(spec.shape[0]):
                part = s[:, lane * 128:(lane + 1) * 128]
                spec[lane, pl.ds(v, bins, stride=2 * GROUP), :] = part[:bins]
                spec[lane, pl.ds(v + GROUP, bins, stride=2 * GROUP), :] = part[bins:]
            return 0

        lax.fori_loop(0, GROUP, one_window, 0, unroll=4)
        for lane in range(spec.shape[0]):
            own[i, :, :, lane * 128:(lane + 1) * 128] = spec[lane].astype(jnp.bfloat16).reshape(
                own.shape[1], own.shape[2], 128)
        if i == 0:
            pl.semaphore_wait(barrier, 2 + ends)
        for way in (UP, DOWN, PARTNER):
            send(way, own.at[i], r, mine + i)
        for way in (RIGHT, LEFT, SIBLING):
            send(way, own.at[i], rows + q, mine + i)
        keep = pltpu.make_async_copy(own.at[i], sets.at[r, mine + i], local_sem.at[i])
        keep.start()
        keeps.append(keep)

    def relay(cond, slot, g, ways):
        goes = [send(way, sets.at[slot, g], slot, g, cond) for way in ways]

        def go():
            arrived(slot, g)
            for f in goes:
                f()

        pl.when(cond)(go)

    def along_x(g):
        for d in range(1, chips):
            relay(x - d >= 0, rows + q - 2 * d, g, (RIGHT, SIBLING))
            relay(x + d < chips, rows + q + 2 * d, g, (LEFT, SIBLING))

    def extra(up, down):
        g = theirs + groups - 1
        for way, cond in ((UP, up), (DOWN, down)):
            pl.when(cond)(send(way, sets.at[r, g], r, g, cond))

    for h in range(1, rows):
        for i in range(groups):
            shared = () if h == 1 and i == groups - 1 else (PARTNER,)
            relay(r - h >= 0, r - h, mine + i, (UP,) + shared)
            relay(r + h < rows, r + h, mine + i, (DOWN,) + shared)
            if h == 1:
                arrived(r, theirs + i)
                for way in (RIGHT, LEFT, SIBLING):
                    send(way, sets.at[r, theirs + i], rows + q, theirs + i)
            if h == 1 and i == groups - 1:
                extra(r < rows - 2, r > 1)
        if h == 1:
            for i in range(groups):
                along_x(mine + i)
        if h == max(1, rows - 2):
            for i in range(groups):
                along_x(theirs + i)
    extra(r == rows - 2, r == 1)

    for h in range(1, rows):
        for i in range(groups):
            pl.when(r - h >= 0)(lambda h=h, i=i: arrived(r - h, theirs + i))
            pl.when(r + h < rows)(lambda h=h, i=i: arrived(r + h, theirs + i))
    for c in range(chips):
        for g in range(2 * groups):
            arrived(rows + 2 * c + 1 - q % 2, g)
    for keep in keeps:
        keep.wait()
    for cond, done in pending:
        if cond is None:
            done()
        else:
            pl.when(cond)(done)


def gather(records, tables, rows, cols):
    windows, channels, length = records.shape
    groups = windows // GROUP
    entries = 2 * tables[0].shape[0]
    bins = entries // 2
    slots = rows + cols
    return pl.pallas_call(
        functools.partial(gather_kernel, rows, cols, groups),
        out_shape=jax.ShapeDtypeStruct(
            (slots, 2 * groups, bins, 2 * GROUP, channels), jnp.bfloat16),
        in_specs=[pl.BlockSpec(memory_space=pl.ANY)] + [pl.BlockSpec(memory_space=pltpu.VMEM)] * 2,
        out_specs=pl.BlockSpec(memory_space=pl.ANY),
        scratch_shapes=[
            pltpu.VMEM(records.shape, jnp.bfloat16),
            pltpu.VMEM((channels // 128, entries * GROUP, 128), jnp.float32),
            pltpu.VMEM((groups, bins, 2 * GROUP, channels), jnp.bfloat16),
            pltpu.SemaphoreType.DMA((groups,)),
            pltpu.SemaphoreType.DMA((groups,)),
            pltpu.SemaphoreType.DMA((6, slots, 2 * groups)),
            pltpu.SemaphoreType.DMA((slots, 2 * groups)),
        ],
        compiler_params=pltpu.CompilerParams(
            collective_id=0, has_side_effects=True, vmem_limit_bytes=40 * 2**20),
        cost_estimate=pl.CostEstimate(
            flops=2 * windows * channels * length * entries,
            bytes_accessed=windows * channels * length * 2, transcendentals=0),
    )(records, *tables)


def cross_kernel(rows, owned, pairs, count, place, sets, out, ring, sem):
    depth, _, step, channels, _ = ring.shape
    groups = sets.shape[1]
    chunks = out.shape[4] // step

    def copy(n):
        part = pl.ds((n % chunks) * step, step)
        return pltpu.make_async_copy(
            ring.at[n % depth], out.at[0, 0, n // chunks, :, part], sem.at[n % depth])

    def one(n, _):
        slot = n % depth
        position = place[0] + n // chunks
        i, j = pairs[0, 0, 0, position], pairs[0, 0, 1, position]
        first = jnp.where(i == place[2], place[1], rows + i)
        live = position < count[0]

        @pl.when(n >= depth)
        def _():
            copy(n - depth).wait()

        @pl.when(live)
        def _():
            for t in range(step):
                k = (n % chunks) * step + t
                a = sets[first, :, k].reshape(-1, channels)
                b = sets[j, :, k].reshape(a.shape)
                parts = b.astype(jnp.float32).reshape(groups, 2, GROUP, channels)
                turned = jnp.concatenate([-parts[:, 1:], parts[:, :1]], axis=1)
                turned = turned.reshape(a.shape).astype(jnp.bfloat16)
                both = lax.dot_general(
                    a, jnp.concatenate([b, turned], axis=1), (((0,), (0,)), ((), ())),
                    preferred_element_type=jnp.float32)
                ring[slot, 0, t] = both[:, :channels].astype(jnp.bfloat16)
                ring[slot, 1, t] = both[:, channels:].astype(jnp.bfloat16)

        @pl.when(jnp.logical_not(live))
        def _():
            ring[slot] = jnp.zeros(ring.shape[1:], jnp.bfloat16)

        copy(n).start()
        return 0

    total = owned * chunks
    lax.fori_loop(0, total, one, 0)
    for n in range(max(total - depth, 0), total):
        copy(n).wait()


def cross(sets, pairs, count, place, rows, owned):
    _, groups, bins, entries, channels = sets.shape
    step = math.gcd(bins, 8)
    smem = pl.BlockSpec(memory_space=pltpu.SMEM)
    return pl.pallas_call(
        functools.partial(cross_kernel, rows, owned),
        out_shape=jax.ShapeDtypeStruct(
            (1, 1, owned, 2, bins, channels, channels), jnp.bfloat16),
        in_specs=[smem, smem, smem, pl.BlockSpec(memory_space=pltpu.VMEM)],
        out_specs=pl.BlockSpec(memory_space=pl.ANY),
        scratch_shapes=[
            pltpu.VMEM((4, 2, step, channels, channels), jnp.bfloat16),
            pltpu.SemaphoreType.DMA((4,)),
        ],
        compiler_params=pltpu.CompilerParams(vmem_limit_bytes=40 * 2**20),
        cost_estimate=pl.CostEstimate(
            flops=4 * owned * bins * channels * channels * groups * entries,
            bytes_accessed=4 * owned * bins * channels * channels, transcendentals=0),
    )(pairs, count, place, sets)


def body(records, tile_pairs, tile_count, bin_index):
    rows, cols = lax.axis_size("row"), lax.axis_size("col")
    r, q = lax.axis_index("row"), lax.axis_index("col")
    sets = gather(records, dft_tables(bin_index, records.shape[2]), rows, cols)
    owned = tile_pairs.shape[2] // lax.axis_size("win")
    place = jnp.stack([lax.axis_index("win") * owned, r, q]).astype(jnp.int32)
    return cross(sets, jnp.swapaxes(tile_pairs, 2, 3), tile_count.reshape(-1), place, rows, owned)


def solution(mesh):
    return jax.shard_map(
        body,
        mesh=mesh,
        in_specs=(
            P("win", ("row", "col"), None),
            P("row", "col", None, None),
            P("row", "col"),
            P(),
        ),
        out_specs=P("row", "col", "win", None, None, None, None),
        check_vma=False,
    )
```

profile of v0, /device:TPU:0, one launch (start us, length us, event | category | flops | bytes accessed | tf_op | source)
XLA Modules:
  0.0 60.3 jit_solution(2626593812538722781)
XLA Ops:
  0.7 0.1 pad_add_fusion.place
  0.8 1.3 %multiply_convert_fusion = (bf16[32,1024]{1,0:T(8,128)(2,1)S(1)}, bf16[32,1024]{1,0:T(8,128)(2,1)S(1)}) fusion(f32[1024]{0:T(1024)S(1)} %get-tuple-element.8, s32[32]{0:T(128)} %param.7, f32[1024]{0:T(1024)S(1)} %get-tuple-element.7), kind=kLoop, calls=%fused_computation.6 | loop fusion | flops 589824 | bytes 139392 | tf_op jit(solution)/shard_map/convert_element_type | solution.py:22
  2.0 0.0 copy-start
  2.0 50.8 %shard_map.46.sets = bf16[8,4,32,16,256]{4,3,2,1,0:T(8,128)(2,1)S(1)} custom-call(bf16[16,256,1024]{2,1,0:T(8,128)(2,1)} %rec_hbm.1, bf16[32,1024]{1,0:T(8,128)(2,1)S(1)} %get-tuple-element.6.cos_ref, bf16[32,1024]{1,0:T(8,128)(2,1)S(1)} %get-tuple-element.5.sin_ref), custom_call_target="tpu_custom_call" | custom-call | flops 536870912 | bytes 8388608 | tf_op jit(solution)/shard_map/pallas_call | solution.py:176
  52.9 0.0 copy-done
  52.9 7.4 %shard_map.47 = bf16[1,1,2,2,32,256,256]{6,5,4,3,2,1,0:T(8,128)(2,1)} custom-call(s32[1,1,2,4]{3,2,1,0:T(2,128)S(1)} %bitcast.6, s32[1]{0:T(128)} %bitcast.5.count, s32[3]{0:T(128)S(1)} %pad_add_fusion.place, bf16[8,4,32,16,256]{4,3,2,1,0:T(8,128)(2,1)S(1)} %shard_map.46.sets), custom_call_target="tpu_custom_call" | custom-call | flops 1073741824 | bytes 16777216 | tf_op jit(solution)/shard_map/pallas_call | solution.py:252
  (1 shorter events, 0.0 us)
Async XLA Ops:
  2.0 50.8 %copy-start = (s32[1,1,4,2]{2,3,1,0:T(2,128)S(1)}, s32[1,1,4,2]{2,3,1,0:T(2,128)}, u32[]{:S(2)}) copy-start(s32[1,1,4,2]{2,3,1,0:T(2,128)} %param.5) | copy-start | bytes 100
where the time goes:
time: 60.7 us; the launch traced here: 60.3 us
  Pallas kernels  58.2 us (96%)
  other arithmetic  1.38 us (2%)
  between operations  0.68 us (1%)
    pallas_call x1, Pallas kernels, gather(): pl.pallas_call(functools.partial(gather_kernel, rows, cols, groups), out_...  50.8 us
    pallas_call x1, Pallas kernels, cross(): pl.pallas_call(functools.partial(cross_kernel, rows, owned), out_shape=ja...  7.42 us
    convert_element_type x1, other arithmetic, dft_tables(): return (cosine.astype(jnp.bfloat16), sine.astype(jnp.bfloat16))  1.26 us

commit v1 on v0

v1 whole, which is shorter than its diff:
```python
import functools
import math

import jax
import jax.numpy as jnp
from jax import lax
from jax.experimental import pallas as pl
from jax.experimental.pallas import tpu as pltpu
from jax.sharding import PartitionSpec as P

GROUP = 8
FETCH = 4
UP, DOWN, PARTNER, RIGHT, LEFT, SIBLING = range(6)


def chunk_list(bins):
    size = max(bins // 8, 1)
    return [(k, min(size, bins - k)) for k in range(0, bins, size)]


def cos_sin(phase, length):
    quarter = length // 4
    turn = (phase + quarter // 2) // quarter
    x = (phase - turn * quarter).astype(jnp.float32) * (2.0 * math.pi / length)
    y = x * x
    c = 1.0 + y * (-0.5 + y * (1.0 / 24 + y * (-1.0 / 720 + y * (1.0 / 40320))))
    s = x * (1.0 + y * (-1.0 / 6 + y * (1.0 / 120 + y * (-1.0 / 5040 + y * (1.0 / 362880)))))
    odd = turn % 2 == 1
    cosine, sine = jnp.where(odd, s, c), jnp.where(odd, c, s)
    turn = turn % 4
    cosine = jnp.where((turn == 1) | (turn == 2), -cosine, cosine)
    sine = jnp.where(turn >= 2, -sine, sine)
    return cosine, sine


def fill_table(bin_ref, kcol, table, length):
    bins = kcol.shape[0]
    for k in range(bins):
        kcol[k:k + 1, :] = jnp.full((1, 128), bin_ref[k], jnp.int32)
    for lane in range(0, length, 128):
        samples = lax.broadcasted_iota(jnp.int32, (8, 128), 1) + lane
        taper = 0.5 - 0.5 * cos_sin(samples, length)[0]
        taper = jnp.concatenate([taper] * (bins // 8), axis=0)
        samples = jnp.concatenate([samples] * (bins // 8), axis=0)
        cosine, sine = cos_sin(kcol[...] * samples % length, length)
        table[:bins, lane:lane + 128] = (taper * cosine).astype(jnp.bfloat16)
        table[bins:, lane:lane + 128] = (-taper * sine).astype(jnp.bfloat16)


def gather_kernel(rows, cols, chunks, pairs, bin_ref, rec_hbm, row_set, col_pick,
                  kcol, table, rec, spec, own, stage, *rest):
    col = rest[:len(chunks)]
    (rec_sem, local_sem, row_send, row_recv, hop_send, hop_recv, pick_send, pick_recv,
     pick_local) = rest[len(chunks):]
    groups, bins = own.shape[0], own.shape[1]
    owned = stage.shape[1]
    w, r, q = lax.axis_index("win"), lax.axis_index("row"), lax.axis_index("col")
    chips = cols // 2
    x = q // 2
    other = 1 - w
    device = {
        UP: (w, r + 1, q), DOWN: (w, r - 1, q), PARTNER: (other, r, q),
        RIGHT: (w, r, q + 2), LEFT: (w, r, q - 2), SIBLING: (w, r, q + 1 - 2 * (q % 2)),
    }
    exists = {
        UP: r < rows - 1, DOWN: r > 0, PARTNER: None,
        RIGHT: x < chips - 1, LEFT: x > 0, SIBLING: None,
    }

    def fetch(i):
        part = pl.ds(i * FETCH, FETCH)
        return pltpu.make_async_copy(rec_hbm.at[part], rec.at[part], rec_sem.at[i])

    for i in range(groups * GROUP // FETCH):
        fetch(i).start()

    def guarded(way, f):
        if exists[way] is None:
            f()
        else:
            pl.when(exists[way])(f)

    barrier = pltpu.get_barrier_semaphore()
    for way in range(6):
        guarded(way, lambda way=way: pl.semaphore_signal(
            barrier, inc=1, device_id=device[way], device_id_type=pl.DeviceIdType.MESH))
    ends = sum(exists[way].astype(jnp.int32) for way in (UP, DOWN, RIGHT, LEFT))

    pending = []

    def send(way, make, cond=None):
        def go():
            guarded(way, lambda: make().start())

        def done():
            guarded(way, lambda: make().wait_send())

        if cond is None:
            go()
        pending.append((cond, done))
        return go

    def remote(way, src, dst, send_sem, recv_sem):
        return pltpu.make_async_remote_copy(
            src_ref=src, dst_ref=dst, send_sem=send_sem, recv_sem=recv_sem,
            device_id=device[way], device_id_type=pl.DeviceIdType.MESH)

    def row_copy(way, src, slot, part):
        return remote(way, src, row_set.at[slot, part],
                      row_send.at[way, slot, part], row_recv.at[slot, part])

    def row_arrived(slot, part):
        row_copy(PARTNER, row_set.at[slot, part], slot, part).wait_recv()

    def row_relay(cond, slot, part, ways):
        goes = [send(way, lambda way=way: row_copy(way, row_set.at[slot, part], slot, part), cond)
                for way in ways]

        def go():
            row_arrived(slot, part)
            for f in goes:
                f()

        pl.when(cond)(go)

    def along_x(part):
        for d in range(1, chips):
            row_relay(x - d >= 0, q - 2 * d, part, (RIGHT, SIBLING))
            row_relay(x + d < chips, q + 2 * d, part, (LEFT, SIBLING))

    def from_partner(g):
        part = groups + g
        row_arrived(q, part)
        for way in (RIGHT, LEFT, SIBLING):
            send(way, lambda way=way: row_copy(way, row_set.at[q, part], q, part))

    def own_hop(way, c, g):
        k, n = chunks[c]
        return remote(way, own.at[g, pl.ds(k, n)], col[c].at[r, g],
                      hop_send.at[way, r, c, g], hop_recv.at[r, c, g])

    def later_hop(way, slot, c):
        return remote(way, col[c].at[slot], col[c].at[slot],
                      hop_send.at[way, slot, c, 0], hop_recv.at[slot, c, 0])

    def hop(h, c):
        for cond, slot, way in ((r - h >= 0, r - h, UP), (r + h < rows, r + h, DOWN)):
            go_on = send(way, lambda slot=slot, way=way: later_hop(way, slot, c), cond)

            def go(slot=slot, go_on=go_on):
                if h == 1:
                    for g in range(groups):
                        remote(PARTNER, own.at[g, pl.ds(*chunks[c])], col[c].at[slot, g],
                               hop_send.at[0, slot, c, g], hop_recv.at[slot, c, g]).wait_recv()
                else:
                    later_hop(PARTNER, slot, c).wait_recv()
                go_on()

            pl.when(cond)(go)

    def pick_copy(c):
        k, n = chunks[c]
        return remote(PARTNER, stage.at[1, :, :, pl.ds(k, n)],
                      col_pick.at[:, pl.ds(groups, groups), pl.ds(k, n)],
                      pick_send.at[c], pick_recv.at[c])

    def pick_keep(c):
        k, n = chunks[c]
        return pltpu.make_async_copy(
            stage.at[0, :, :, pl.ds(k, n)],
            col_pick.at[:, pl.ds(0, groups), pl.ds(k, n)], pick_local.at[c])

    def pick(c):
        k, n = chunks[c]
        for side, half in ((1, other), (0, w)):
            for t in range(owned):
                j = pairs[0, 0, 1, half * owned + t]
                stage[side, t, :, k:k + n] = col[c][j]
            if side:
                send(PARTNER, lambda: pick_copy(c))
            else:
                pick_keep(c).start()

    fill_table(bin_ref, kcol, table, rec.shape[2])
    keeps = []
    for g in range(groups):
        for i in range(g * GROUP // FETCH, (g + 1) * GROUP // FETCH):
            fetch(i).wait()
            for v in range(i * FETCH, (i + 1) * FETCH):
                s = lax.dot_general(table[...], rec[v], (((1,), (1,)), ((), ())),
                                    preferred_element_type=jnp.float32)
                scale = 1.0 / jnp.sqrt(jnp.mean(s * s, axis=0, keepdims=True) + 1e-06)
                s = s * scale
                first = v % GROUP
                for lane in range(spec.shape[0]):
                    part = s[:, lane * 128:(lane + 1) * 128]
                    spec[lane, pl.ds(first, bins, stride=2 * GROUP), :] = part[:bins]
                    spec[lane, pl.ds(first + GROUP, bins, stride=2 * GROUP), :] = part[bins:]
        for lane in range(spec.shape[0]):
            part = spec[lane].astype(jnp.bfloat16).reshape(bins, 2 * GROUP, 128)
            own[g, :, :, lane * 128:(lane + 1) * 128] = part
            for c, (k, n) in enumerate(chunks):
                col[c][r, g, :, :, lane * 128:(lane + 1) * 128] = part[k:k + n]
        if g == 0:
            pl.semaphore_wait(barrier, 2 + ends)
        for c in range(len(chunks)):
            for way in (UP, DOWN):
                send(way, lambda way=way, c=c, g=g: own_hop(way, c, g))
            if c == 0:
                send(PARTNER, lambda g=g: remote(
                    PARTNER, own.at[g], row_set.at[q, groups + g],
                    row_send.at[PARTNER, q, groups + g], row_recv.at[q, groups + g]))
                for way in (RIGHT, LEFT, SIBLING):
                    send(way, lambda way=way, g=g: row_copy(way, own.at[g], q, g))
        keep = pltpu.make_async_copy(own.at[g], row_set.at[q, g], local_sem.at[g])
        keep.start()
        keeps.append(keep)

    last = len(chunks) + rows - 2
    for step in range(last):
        for h in range(1, rows):
            if 0 <= step - h + 1 < len(chunks):
                hop(h, step - h + 1)
        done = step - rows + 2
        if done >= 0:
            pick(done)
        if done == 1:
            for g in range(groups):
                from_partner(g)
                along_x(g)
        if done == len(chunks) // 2 + 1:
            for g in range(groups):
                along_x(groups + g)

    for c in range(chips):
        for part in range(2 * groups):
            row_arrived(2 * c + 1 - q % 2, part)
    for c in range(len(chunks)):
        pick_copy(c).wait_recv()
        pick_keep(c).wait()
    for keep in keeps:
        keep.wait()
    for cond, done in pending:
        if cond is None:
            done()
        else:
            pl.when(cond)(done)


def gather(records, pairs, bin_index, rows, cols, owned):
    windows, channels, length = records.shape
    groups = windows // GROUP
    bins = bin_index.shape[0]
    chunks = chunk_list(bins)
    count = len(chunks)
    smem = pl.BlockSpec(memory_space=pltpu.SMEM)
    hbm = pl.BlockSpec(memory_space=pl.ANY)
    dma = pltpu.SemaphoreType.DMA
    tile = (2 * GROUP, channels)
    return pl.pallas_call(
        functools.partial(gather_kernel, rows, cols, chunks),
        out_shape=(
            jax.ShapeDtypeStruct((cols, 2 * groups, bins) + tile, jnp.bfloat16),
            jax.ShapeDtypeStruct((owned, 2 * groups, bins) + tile, jnp.bfloat16)),
        in_specs=[smem, smem, hbm],
        out_specs=(hbm, hbm),
        scratch_shapes=[
            pltpu.VMEM((bins, 128), jnp.int32),
            pltpu.VMEM((2 * bins, length), jnp.bfloat16),
            pltpu.VMEM(records.shape, jnp.bfloat16),
            pltpu.VMEM((channels // 128, 2 * bins * GROUP, 128), jnp.float32),
            pltpu.VMEM((groups, bins) + tile, jnp.bfloat16),
            pltpu.VMEM((2, owned, groups, bins) + tile, jnp.bfloat16),
            *[pltpu.VMEM((rows, groups, n) + tile, jnp.bfloat16) for _, n in chunks],
            dma((windows // FETCH,)),
            dma((groups,)),
            dma((6, cols, 2 * groups)),
            dma((cols, 2 * groups)),
            dma((2, rows, count, groups)),
            dma((rows, count, groups)),
            dma((count,)),
            dma((count,)),
            dma((count,)),
        ],
        compiler_params=pltpu.CompilerParams(
            collective_id=0, has_side_effects=True, vmem_limit_bytes=40 * 2**20),
        cost_estimate=pl.CostEstimate(
            flops=4 * windows * channels * length * bins,
            bytes_accessed=windows * channels * length * 2, transcendentals=0),
    )(pairs, bin_index, records)


def cross_kernel(owned, pairs, count, place, row_set, col_pick, out, ring, sem):
    depth, _, step, channels, _ = ring.shape
    groups = row_set.shape[1]
    chunks = out.shape[4] // step

    def copy(n):
        part = pl.ds((n % chunks) * step, step)
        return pltpu.make_async_copy(
            ring.at[n % depth], out.at[0, 0, n // chunks, :, part], sem.at[n % depth])

    def one(n, _):
        slot = n % depth
        position = place[0] * owned + n // chunks
        i = pairs[0, 0, 0, position]
        live = position < count[0]

        @pl.when(n >= depth)
        def _():
            copy(n - depth).wait()

        @pl.when(live)
        def _():
            for t in range(step):
                k = (n % chunks) * step + t
                a = row_set[i, :, k].reshape(-1, channels)
                b = col_pick[n // chunks, :, k].reshape(a.shape)
                parts = b.astype(jnp.float32).reshape(groups, 2, GROUP, channels)
                turned = jnp.concatenate([-parts[:, 1:], parts[:, :1]], axis=1)
                turned = turned.reshape(a.shape).astype(jnp.bfloat16)
                both = lax.dot_general(
                    a, jnp.concatenate([b, turned], axis=1), (((0,), (0,)), ((), ())),
                    preferred_element_type=jnp.float32)
                ring[slot, 0, t] = both[:, :channels].astype(jnp.bfloat16)
                ring[slot, 1, t] = both[:, channels:].astype(jnp.bfloat16)

        @pl.when(jnp.logical_not(live))
        def _():
            ring[slot] = jnp.zeros(ring.shape[1:], jnp.bfloat16)

        copy(n).start()
        return 0

    total = owned * chunks
    lax.fori_loop(0, total, one, 0)
    for n in range(max(total - depth, 0), total):
        copy(n).wait()


def cross(row_set, col_pick, pairs, count, place):
    owned, groups, bins, entries, channels = col_pick.shape
    step = math.gcd(bins, 8)
    smem = pl.BlockSpec(memory_space=pltpu.SMEM)
    vmem = pl.BlockSpec(memory_space=pltpu.VMEM)
    return pl.pallas_call(
        functools.partial(cross_kernel, owned),
        out_shape=jax.ShapeDtypeStruct(
            (1, 1, owned, 2, bins, channels, channels), jnp.bfloat16),
        in_specs=[smem, smem, smem, vmem, vmem],
        out_specs=pl.BlockSpec(memory_space=pl.ANY),
        scratch_shapes=[
            pltpu.VMEM((4, 2, step, channels, channels), jnp.bfloat16),
            pltpu.SemaphoreType.DMA((4,)),
        ],
        compiler_params=pltpu.CompilerParams(vmem_limit_bytes=40 * 2**20),
        cost_estimate=pl.CostEstimate(
            flops=4 * owned * bins * channels * channels * groups * entries,
            bytes_accessed=4 * owned * bins * channels * channels, transcendentals=0),
    )(pairs, count, place, row_set, col_pick)


def body(records, tile_pairs, tile_count, bin_index):
    rows, cols = lax.axis_size("row"), lax.axis_size("col")
    owned = tile_pairs.shape[2] // lax.axis_size("win")
    pairs = jnp.swapaxes(tile_pairs, 2, 3)
    row_set, col_pick = gather(records, pairs, bin_index, rows, cols, owned)
    place = lax.axis_index("win").astype(jnp.int32).reshape(1)
    return cross(row_set, col_pick, pairs, tile_count.reshape(-1), place)


def solution(mesh):
    return jax.shard_map(
        body,
        mesh=mesh,
        in_specs=(
            P("win", ("row", "col"), None),
            P("row", "col", None, None),
            P("row", "col"),
            P(),
        ),
        out_specs=P("row", "col", "win", None, None, None, None),
        check_vma=False,
    )
```

time: 60.7 us -> 61.6 us (1.015)
  other arithmetic: 1.38 us -> 0 us
  local copies, waits for them, and re-layouts: 0.01 us -> 1.33 us
  Pallas kernels: 58.2 us -> 59.4 us
    unnamed x2 -> x4, local copies, waits for them, and re-layouts: 0.01 us -> 1.33 us
    convert_element_type x1 -> x0, other arithmetic: 1.26 us -> none  [dft_tables(): return (cosine.astype(jnp.bfloat16), sine.astype(jnp.bfloat16))]
    pallas_call x2, Pallas kernels: 58.2 us -> 59.4 us  [the longest x1 51.5 us: gather(): pl.pallas_call(functools.partial(gather_kernel, rows, cols, chunks), out_...]
where the time goes in v1:
time: 61.6 us; the launch traced here: 61.4 us
  Pallas kernels  59.4 us (96%)
  local copies, waits for them, and re-layouts  1.33 us (2%)
  between operations  0.67 us (1%)
    pallas_call x1, Pallas kernels, gather(): pl.pallas_call(functools.partial(gather_kernel, rows, cols, chunks), out_...  51.5 us
    pallas_call x1, Pallas kernels, cross(): pl.pallas_call(functools.partial(cross_kernel, owned), out_shape=jax.Shap...  7.9 us
    unnamed x4, local copies, waits for them, and re-layouts  1.33 us

profile of v1, /device:TPU:0, one launch (start us, length us, event | category | flops | bytes accessed | tf_op | source)
XLA Modules:
  0.0 61.4 jit_solution(87160593274451199)
XLA Ops:
  0.7 0.0 copy-start
  0.7 0.7 %copy-done = s32[1,1,4,2]{2,3,1,0:T(2,128)S(1)} copy-done((s32[1,1,4,2]{2,3,1,0:T(2,128)S(1)}, s32[1,1,4,2]{2,3,1,0:T(2,128)}, u32[]{:S(2)}) %copy-start) | copy-done | bytes 56
  1.3 0.0 copy-start.1
  1.3 0.7 %copy-done.1 = s32[32]{0:T(128)S(1)} copy-done((s32[32]{0:T(128)S(1)}, s32[32]{0:T(128)}, u32[]{:S(2)}) %copy-start.1) | copy-done | bytes 152
  2.0 51.5 %shard_map.46 = (bf16[4,4,32,16,256]{4,3,2,1,0:T(8,128)(2,1)S(1)}, bf16[2,4,32,16,256]{4,3,2,1,0:T(8,128)(2,1)S(1)}) custom-call(s32[1,1,2,4]{3,2,1,0:T(2,128)S(1)} %bitcast.4, s32[32]{0:T(128)S(1)} %copy-done.1, bf16[16,256,1024]{2,1,0:T(8,128)(2,1)} %rec_hbm.1), custom_call_target="tpu_custom_call" | custom-call | flops 536870912 | bytes 8388608 | tf_op jit(solution)/shard_map/pallas_call | solution.py:260
  53.5 7.9 %shard_map.47 = bf16[1,1,2,2,32,256,256]{6,5,4,3,2,1,0:T(8,128)(2,1)} custom-call(s32[1,1,2,4]{3,2,1,0:T(2,128)S(1)} %bitcast.5, s32[1]{0:T(128)} %bitcast.3.count, s32[1]{0:T(128)} %bitcast.2.place, bf16[4,4,32,16,256]{4,3,2,1,0:T(8,128)(2,1)S(1)} %get-tuple-element.7.row_set, bf16[2,4,32,16,256]{4,3,2,1,0:T(8,128)(2,1)S(1)} %get-tuple-element.8.col_pick), custom_call_target="tpu_custom_call" | custom-call | flops 1073741824 | bytes 16777216 | tf_op jit(solution)/shard_map/pallas_call | solution.py:346
Async XLA Ops:
  0.7 0.7 %copy-start = (s32[1,1,4,2]{2,3,1,0:T(2,128)S(1)}, s32[1,1,4,2]{2,3,1,0:T(2,128)}, u32[]{:S(2)}) copy-start(s32[1,1,4,2]{2,3,1,0:T(2,128)} %param.5) | copy-start | bytes 100
  1.3 0.7 %copy-start.1 = (s32[32]{0:T(128)S(1)}, s32[32]{0:T(128)}, u32[]{:S(2)}) copy-start(s32[32]{0:T(128)} %bin_ref.1) | copy-start | bytes 388

commit v2 on v1

--- a/solution.py
+++ b/solution.py
@@ -10,30 +10,35 @@
 
 GROUP = 8
 FETCH = 4
+AHEAD = 4
 UP, DOWN, PARTNER, RIGHT, LEFT, SIBLING = range(6)
 
 
 def chunk_list(bins):
     size = max(bins // 8, 1)
-    return [(k, min(size, bins - k)) for k in range(0, bins, size)]
+    ends = list(range(size, bins, size))
+    if size > 1:
+        ends.append(bins - size // 2)
+    ends.append(bins)
+    return [(a, b - a) for a, b in zip([0] + ends, ends)]
 
 
 def cos_sin(phase, length):
-    quarter = length // 4
-    turn = (phase + quarter // 2) // quarter
-    x = (phase - turn * quarter).astype(jnp.float32) * (2.0 * math.pi / length)
+    shift = length.bit_length() - 3
+    turn = (phase + (1 << shift >> 1)) >> shift
+    x = (phase - (turn << shift)).astype(jnp.float32) * (2.0 * math.pi / length)
     y = x * x
     c = 1.0 + y * (-0.5 + y * (1.0 / 24 + y * (-1.0 / 720 + y * (1.0 / 40320))))
     s = x * (1.0 + y * (-1.0 / 6 + y * (1.0 / 120 + y * (-1.0 / 5040 + y * (1.0 / 362880)))))
-    odd = turn % 2 == 1
+    odd = (turn & 1) == 1
     cosine, sine = jnp.where(odd, s, c), jnp.where(odd, c, s)
-    turn = turn % 4
-    cosine = jnp.where((turn == 1) | (turn == 2), -cosine, cosine)
-    sine = jnp.where(turn >= 2, -sine, sine)
+    cosine = jnp.where(((turn + 1) & 2) == 2, -cosine, cosine)
+    sine = jnp.where((turn & 2) == 2, -sine, sine)
     return cosine, sine
 
 
 def fill_table(bin_ref, kcol, table, length):
+    assert length & (length - 1) == 0
     bins = kcol.shape[0]
     for k in range(bins):
         kcol[k:k + 1, :] = jnp.full((1, 128), bin_ref[k], jnp.int32)
@@ -42,16 +47,16 @@
         taper = 0.5 - 0.5 * cos_sin(samples, length)[0]
         taper = jnp.concatenate([taper] * (bins // 8), axis=0)
         samples = jnp.concatenate([samples] * (bins // 8), axis=0)
-        cosine, sine = cos_sin(kcol[...] * samples % length, length)
+        cosine, sine = cos_sin(kcol[...] * samples & (length - 1), length)
         table[:bins, lane:lane + 128] = (taper * cosine).astype(jnp.bfloat16)
         table[bins:, lane:lane + 128] = (-taper * sine).astype(jnp.bfloat16)
 
 
-def gather_kernel(rows, cols, chunks, pairs, bin_ref, rec_hbm, row_set, col_pick,
-                  kcol, table, rec, spec, own, stage, *rest):
+def gather_kernel(rows, cols, chunks, pairs_hbm, bin_hbm, rec_hbm, row_set, col_pick,
+                  pairs, bin_ref, scalar_sem, kcol, table, rec, spec, own, stage, *rest):
     col = rest[:len(chunks)]
-    (rec_sem, local_sem, row_send, row_recv, hop_send, hop_recv, pick_send, pick_recv,
-     pick_local) = rest[len(chunks):]
+    (rec_sem, local_sem, partner_send, row_send, row_recv, sibling_recv, hop_send, hop_recv,
+     pick_sem) = rest[len(chunks):]
     groups, bins = own.shape[0], own.shape[1]
     owned = stage.shape[1]
     w, r, q = lax.axis_index("win"), lax.axis_index("row"), lax.axis_index("col")
@@ -71,6 +76,10 @@
         part = pl.ds(i * FETCH, FETCH)
         return pltpu.make_async_copy(rec_hbm.at[part], rec.at[part], rec_sem.at[i])
 
+    scalars = [pltpu.make_async_copy(bin_hbm, bin_ref, scalar_sem.at[0]),
+               pltpu.make_async_copy(pairs_hbm, pairs, scalar_sem.at[1])]
+    for scalar in scalars:
+        scalar.start()
     for i in range(groups * GROUP // FETCH):
         fetch(i).start()
 
@@ -86,40 +95,26 @@
             barrier, inc=1, device_id=device[way], device_id_type=pl.DeviceIdType.MESH))
     ends = sum(exists[way].astype(jnp.int32) for way in (UP, DOWN, RIGHT, LEFT))
 
-    pending = []
-
-    def send(way, make, cond=None):
-        def go():
-            guarded(way, lambda: make().start())
-
-        def done():
-            guarded(way, lambda: make().wait_send())
-
-        if cond is None:
-            go()
-        pending.append((cond, done))
-        return go
-
     def remote(way, src, dst, send_sem, recv_sem):
         return pltpu.make_async_remote_copy(
             src_ref=src, dst_ref=dst, send_sem=send_sem, recv_sem=recv_sem,
             device_id=device[way], device_id_type=pl.DeviceIdType.MESH)
 
+    def start(way, copy):
+        guarded(way, copy.start)
+
     def row_copy(way, src, slot, part):
-        return remote(way, src, row_set.at[slot, part],
-                      row_send.at[way, slot, part], row_recv.at[slot, part])
+        recv = sibling_recv.at[slot // 2] if way == SIBLING else row_recv.at[slot // 2, part]
+        return remote(way, src, row_set.at[slot, part], row_send.at[way - RIGHT, slot], recv)
 
     def row_arrived(slot, part):
-        row_copy(PARTNER, row_set.at[slot, part], slot, part).wait_recv()
+        row_copy(RIGHT, row_set.at[slot, part], slot, part).wait_recv()
 
     def row_relay(cond, slot, part, ways):
-        goes = [send(way, lambda way=way: row_copy(way, row_set.at[slot, part], slot, part), cond)
-                for way in ways]
-
         def go():
             row_arrived(slot, part)
-            for f in goes:
-                f()
+            for way in ways:
+                start(way, row_copy(way, row_set.at[slot, part], slot, part))
 
         pl.when(cond)(go)
 
@@ -128,47 +123,73 @@
             row_relay(x - d >= 0, q - 2 * d, part, (RIGHT, SIBLING))
             row_relay(x + d < chips, q + 2 * d, part, (LEFT, SIBLING))
 
+    def to_partner(g):
+        return remote(PARTNER, own.at[g], row_set.at[q, groups + g],
+                      partner_send.at[0], row_recv.at[q // 2, groups + g])
+
     def from_partner(g):
         part = groups + g
         row_arrived(q, part)
         for way in (RIGHT, LEFT, SIBLING):
-            send(way, lambda way=way: row_copy(way, row_set.at[q, part], q, part))
-
-    def own_hop(way, c, g):
+            start(way, row_copy(way, row_set.at[q, part], q, part))
+
+    def rows_done():
+        def slot_bytes(way, slot):
+            return remote(way, row_set.at[slot], row_set.at[slot],
+                          row_send.at[way - RIGHT, slot], sibling_recv.at[slot // 2])
+
+        remote(PARTNER, own, own, partner_send.at[0], partner_send.at[0]).wait_send()
+        for way in (RIGHT, LEFT, SIBLING):
+            guarded(way, slot_bytes(way, q).wait_send)
+        for d in range(1, chips):
+            for cond, slot, way in ((x - d >= 0, q - 2 * d, RIGHT), (x + d < chips, q + 2 * d, LEFT)):
+                def done(slot=slot, way=way):
+                    guarded(way, slot_bytes(way, slot).wait_send)
+                    slot_bytes(SIBLING, slot).wait_send()
+
+                pl.when(cond)(done)
+        for c in range(chips):
+            slot_bytes(SIBLING, 2 * c + 1 - q % 2).wait_recv()
+
+    def hop_copy(way, slot, c, src, dst):
+        return remote(way, src, dst, hop_send.at[way, slot],
+                      hop_recv.at[slot - (1 if way == DOWN else 0), c])
+
+    def send_own(c, g=None):
         k, n = chunks[c]
-        return remote(way, own.at[g, pl.ds(k, n)], col[c].at[r, g],
-                      hop_send.at[way, r, c, g], hop_recv.at[r, c, g])
-
-    def later_hop(way, slot, c):
-        return remote(way, col[c].at[slot], col[c].at[slot],
-                      hop_send.at[way, slot, c, 0], hop_recv.at[slot, c, 0])
+        for way in (UP, DOWN):
+            if g is None:
+                copy = hop_copy(way, r, c, own.at[:, pl.ds(k, n)], col[c].at[r])
+            else:
+                copy = hop_copy(way, r, c, own.at[g, pl.ds(k, n)], col[c].at[r, g])
+            start(way, copy)
 
     def hop(h, c):
         for cond, slot, way in ((r - h >= 0, r - h, UP), (r + h < rows, r + h, DOWN)):
-            go_on = send(way, lambda slot=slot, way=way: later_hop(way, slot, c), cond)
-
-            def go(slot=slot, go_on=go_on):
-                if h == 1:
-                    for g in range(groups):
-                        remote(PARTNER, own.at[g, pl.ds(*chunks[c])], col[c].at[slot, g],
-                               hop_send.at[0, slot, c, g], hop_recv.at[slot, c, g]).wait_recv()
-                else:
-                    later_hop(PARTNER, slot, c).wait_recv()
-                go_on()
+            def go(slot=slot, way=way):
+                copy = hop_copy(way, slot, c, col[c].at[slot], col[c].at[slot])
+                copy.wait_recv()
+                start(way, copy)
 
             pl.when(cond)(go)
 
-    def pick_copy(c):
-        k, n = chunks[c]
-        return remote(PARTNER, stage.at[1, :, :, pl.ds(k, n)],
-                      col_pick.at[:, pl.ds(groups, groups), pl.ds(k, n)],
-                      pick_send.at[c], pick_recv.at[c])
-
-    def pick_keep(c):
-        k, n = chunks[c]
+    def hops_done():
+        for slot_cond, slot, way in [(r >= 0, r, UP), (r >= 0, r, DOWN)] + [
+                item for h in range(1, rows)
+                for item in ((r - h >= 0, r - h, UP), (r + h < rows, r + h, DOWN))]:
+            def done(slot=slot, way=way):
+                guarded(way, remote(way, own, own, hop_send.at[way, slot],
+                                    hop_send.at[way, slot]).wait_send)
+
+            pl.when(slot_cond)(done)
+
+    def pick_copy(part):
+        return remote(PARTNER, stage.at[1, :, :, part], col_pick.at[:, pl.ds(groups, groups), part],
+                      pick_sem.at[0], pick_sem.at[1])
+
+    def pick_keep(part):
         return pltpu.make_async_copy(
-            stage.at[0, :, :, pl.ds(k, n)],
-            col_pick.at[:, pl.ds(0, groups), pl.ds(k, n)], pick_local.at[c])
+            stage.at[0, :, :, part], col_pick.at[:, pl.ds(0, groups), part], pick_sem.at[2])
 
     def pick(c):
         k, n = chunks[c]
@@ -176,13 +197,12 @@
             for t in range(owned):
                 j = pairs[0, 0, 1, half * owned + t]
                 stage[side, t, :, k:k + n] = col[c][j]
-            if side:
-                send(PARTNER, lambda: pick_copy(c))
-            else:
-                pick_keep(c).start()
-
+            (pick_copy if side else pick_keep)(pl.ds(k, n)).start()
+
+    for scalar in scalars:
+        scalar.wait()
     fill_table(bin_ref, kcol, table, rec.shape[2])
-    keeps = []
+    split = min(AHEAD, len(chunks))
     for g in range(groups):
         for i in range(g * GROUP // FETCH, (g + 1) * GROUP // FETCH):
             fetch(i).wait()
@@ -203,48 +223,45 @@
                 col[c][r, g, :, :, lane * 128:(lane + 1) * 128] = part[k:k + n]
         if g == 0:
             pl.semaphore_wait(barrier, 2 + ends)
-        for c in range(len(chunks)):
-            for way in (UP, DOWN):
-                send(way, lambda way=way, c=c, g=g: own_hop(way, c, g))
-            if c == 0:
-                send(PARTNER, lambda g=g: remote(
-                    PARTNER, own.at[g], row_set.at[q, groups + g],
-                    row_send.at[PARTNER, q, groups + g], row_recv.at[q, groups + g]))
-                for way in (RIGHT, LEFT, SIBLING):
-                    send(way, lambda way=way, g=g: row_copy(way, own.at[g], q, g))
-        keep = pltpu.make_async_copy(own.at[g], row_set.at[q, g], local_sem.at[g])
-        keep.start()
-        keeps.append(keep)
+        send_own(0, g)
+        to_partner(g).start()
+        for way in (RIGHT, LEFT, SIBLING):
+            start(way, row_copy(way, own.at[g], q, g))
+        if g == 0:
+            for c in range(1, split):
+                send_own(c, g)
+        elif split > 1:
+            send_own(1, g)
+    keep = pltpu.make_async_copy(own, row_set.at[q, pl.ds(0, groups)], local_sem.at[0])
+    keep.start()
 
     last = len(chunks) + rows - 2
-    for step in range(last):
+    row_work = {}
+    for g in range(groups):
+        row_work[2 + 2 * g] = lambda g=g: from_partner(g)
+        row_work[3 + 2 * g] = lambda g=g: along_x(g)
+        row_work[3 + 2 * groups + g] = lambda g=g: along_x(groups + g)
+    for step in range(max(last, 3 + 3 * groups)):
+        if 2 + step < len(chunks):
+            if 2 + step < split:
+                for g in range(1, groups):
+                    send_own(2 + step, g)
+            else:
+                send_own(2 + step)
         for h in range(1, rows):
             if 0 <= step - h + 1 < len(chunks):
                 hop(h, step - h + 1)
-        done = step - rows + 2
-        if done >= 0:
-            pick(done)
-        if done == 1:
-            for g in range(groups):
-                from_partner(g)
-                along_x(g)
-        if done == len(chunks) // 2 + 1:
-            for g in range(groups):
-                along_x(groups + g)
-
-    for c in range(chips):
-        for part in range(2 * groups):
-            row_arrived(2 * c + 1 - q % 2, part)
-    for c in range(len(chunks)):
-        pick_copy(c).wait_recv()
-        pick_keep(c).wait()
-    for keep in keeps:
-        keep.wait()
-    for cond, done in pending:
-        if cond is None:
-            done()
-        else:
-            pl.when(cond)(done)
+        if 0 <= step - rows + 2 < len(chunks):
+            pick(step - rows + 2)
+        if step in row_work:
+            row_work[step]()
+
+    every = pl.ds(0, bins)
+    rows_done()
+    hops_done()
+    pick_copy(every).wait()
+    pick_keep(every).wait()
+    keep.wait()
 
 
 def gather(records, pairs, bin_index, rows, cols, owned):
@@ -253,7 +270,6 @@
     bins = bin_index.shape[0]
     chunks = chunk_list(bins)
     count = len(chunks)
-    smem = pl.BlockSpec(memory_space=pltpu.SMEM)
     hbm = pl.BlockSpec(memory_space=pl.ANY)
     dma = pltpu.SemaphoreType.DMA
     tile = (2 * GROUP, channels)
@@ -262,9 +278,12 @@
         out_shape=(
             jax.ShapeDtypeStruct((cols, 2 * groups, bins) + tile, jnp.bfloat16),
             jax.ShapeDtypeStruct((owned, 2 * groups, bins) + tile, jnp.bfloat16)),
-        in_specs=[smem, smem, hbm],
+        in_specs=[pl.BlockSpec(memory_space=pltpu.HBM)] * 2 + [hbm],
         out_specs=(hbm, hbm),
         scratch_shapes=[
+            pltpu.SMEM(pairs.shape, jnp.int32),
+            pltpu.SMEM((bins,), jnp.int32),
+            dma((2,)),
             pltpu.VMEM((bins, 128), jnp.int32),
             pltpu.VMEM((2 * bins, length), jnp.bfloat16),
             pltpu.VMEM(records.shape, jnp.bfloat16),
@@ -273,14 +292,14 @@
             pltpu.VMEM((2, owned, groups, bins) + tile, jnp.bfloat16),
             *[pltpu.VMEM((rows, groups, n) + tile, jnp.bfloat16) for _, n in chunks],
             dma((windows // FETCH,)),
-            dma((groups,)),
-            dma((6, cols, 2 * groups)),
-            dma((cols, 2 * groups)),
-            dma((2, rows, count, groups)),
-            dma((rows, count, groups)),
-            dma((count,)),
-            dma((count,)),
-            dma((count,)),
+            dma((1,)),
+            dma((1,)),
+            dma((3, cols)),
+            dma((cols // 2, 2 * groups)),
+            dma((cols // 2,)),
+            dma((2, rows)),
+            dma((rows - 1, count)),
+            dma((3,)),
         ],
         compiler_params=pltpu.CompilerParams(
             collective_id=0, has_side_effects=True, vmem_limit_bytes=40 * 2**20),

time: 61.6 us -> 58.2 us (0.945)
  Pallas kernels: 59.4 us -> 56 us
    pallas_call x1, Pallas kernels: 51.5 us -> 48.1 us  [gather(): pl.pallas_call(functools.partial(gather_kernel, rows, cols, chunks), out_...]
where the time goes in v2:
time: 58.2 us; the launch traced here: 58 us
  Pallas kernels  56 us (96%)
  local copies, waits for them, and re-layouts  1.33 us (2%)
  between operations  0.67 us (1%)
    pallas_call x1, Pallas kernels, gather(): pl.pallas_call(functools.partial(gather_kernel, rows, cols, chunks), out_...  48.1 us
    pallas_call x1, Pallas kernels, cross(): pl.pallas_call(functools.partial(cross_kernel, owned), out_shape=jax.Shap...  7.9 us
    unnamed x4, local copies, waits for them, and re-layouts  1.33 us

profile of v2, /device:TPU:0, one launch (start us, length us, event | category | flops | bytes accessed | tf_op | source)
XLA Modules:
  0.0 58.0 jit_solution(8941190365006626332)
XLA Ops:
  0.7 0.0 copy-start
  0.7 0.7 %copy-done = s32[1,1,4,2]{2,3,1,0:T(2,128)S(1)} copy-done((s32[1,1,4,2]{2,3,1,0:T(2,128)S(1)}, s32[1,1,4,2]{2,3,1,0:T(2,128)}, u32[]{:S(2)}) %copy-start) | copy-done | bytes 56
  1.3 0.0 copy-start.1
  1.3 0.7 %copy-done.1 = s32[32]{0:T(128)S(1)} copy-done((s32[32]{0:T(128)S(1)}, s32[32]{0:T(128)}, u32[]{:S(2)}) %copy-start.1) | copy-done | bytes 152
  2.0 48.1 %shard_map.46 = (bf16[4,4,32,16,256]{4,3,2,1,0:T(8,128)(2,1)S(1)}, bf16[2,4,32,16,256]{4,3,2,1,0:T(8,128)(2,1)S(1)}) custom-call(s32[1,1,2,4]{3,2,1,0:T(2,128)S(1)} %bitcast.4, s32[32]{0:T(128)S(1)} %copy-done.1, bf16[16,256,1024]{2,1,0:T(8,128)(2,1)} %rec_hbm.1), custom_call_target="tpu_custom_call" | custom-call | flops 536870912 | bytes 8388608 | tf_op jit(solution)/shard_map/pallas_call | solution.py:276
  50.1 7.9 %shard_map.47 = bf16[1,1,2,2,32,256,256]{6,5,4,3,2,1,0:T(8,128)(2,1)} custom-call(s32[1,1,2,4]{3,2,1,0:T(2,128)S(1)} %bitcast.5, s32[1]{0:T(128)} %bitcast.3.count, s32[1]{0:T(128)} %bitcast.2.place, bf16[4,4,32,16,256]{4,3,2,1,0:T(8,128)(2,1)S(1)} %get-tuple-element.7.row_set, bf16[2,4,32,16,256]{4,3,2,1,0:T(8,128)(2,1)S(1)} %get-tuple-element.8.col_pick), custom_call_target="tpu_custom_call" | custom-call | flops 1073741824 | bytes 16777216 | tf_op jit(solution)/shard_map/pallas_call | solution.py:365
Async XLA Ops:
  0.7 0.7 %copy-start = (s32[1,1,4,2]{2,3,1,0:T(2,128)S(1)}, s32[1,1,4,2]{2,3,1,0:T(2,128)}, u32[]{:S(2)}) copy-start(s32[1,1,4,2]{2,3,1,0:T(2,128)} %param.5) | copy-start | bytes 100
  1.3 0.7 %copy-start.1 = (s32[32]{0:T(128)S(1)}, s32[32]{0:T(128)}, u32[]{:S(2)}) copy-start(s32[32]{0:T(128)} %bin_hbm.1) | copy-start | bytes 388

commit v3 on v2

--- a/solution.py
+++ b/solution.py
@@ -10,17 +10,15 @@
 
 GROUP = 8
 FETCH = 4
-AHEAD = 4
-UP, DOWN, PARTNER, RIGHT, LEFT, SIBLING = range(6)
+AHEAD = 5
+BOTH = 3
+WINDOW = 2
+UP, DOWN, PARTNER, RIGHT, LEFT, SIBLING, CROSS_UP, CROSS_DOWN = range(8)
 
 
 def chunk_list(bins):
     size = max(bins // 8, 1)
-    ends = list(range(size, bins, size))
-    if size > 1:
-        ends.append(bins - size // 2)
-    ends.append(bins)
-    return [(a, b - a) for a, b in zip([0] + ends, ends)]
+    return [(k, min(size, bins - k)) for k in range(0, bins, size)]
 
 
 def cos_sin(phase, length):
@@ -53,10 +51,11 @@
 
 
 def gather_kernel(rows, cols, chunks, pairs_hbm, bin_hbm, rec_hbm, row_set, col_pick,
-                  pairs, bin_ref, scalar_sem, kcol, table, rec, spec, own, stage, *rest):
+                  pairs, bin_ref, scalar_sem, kcol, table, rec, spec, own, stage,
+                  end_stage, end_arrived, end_pairs, *rest):
     col = rest[:len(chunks)]
-    (rec_sem, local_sem, partner_send, row_send, row_recv, sibling_recv, hop_send, hop_recv,
-     pick_sem) = rest[len(chunks):]
+    (rec_sem, local_sem, partner_send, row_send, row_recv, sibling_recv, hop_send, relay_send, hop_recv,
+     pick_sem, pair_sem, end_send, end_recv) = rest[len(chunks):]
     groups, bins = own.shape[0], own.shape[1]
     owned = stage.shape[1]
     w, r, q = lax.axis_index("win"), lax.axis_index("row"), lax.axis_index("col")
@@ -66,11 +65,18 @@
     device = {
         UP: (w, r + 1, q), DOWN: (w, r - 1, q), PARTNER: (other, r, q),
         RIGHT: (w, r, q + 2), LEFT: (w, r, q - 2), SIBLING: (w, r, q + 1 - 2 * (q % 2)),
+        CROSS_UP: (other, r + 1, q), CROSS_DOWN: (other, r - 1, q),
     }
     exists = {
         UP: r < rows - 1, DOWN: r > 0, PARTNER: None,
         RIGHT: x < chips - 1, LEFT: x > 0, SIBLING: None,
+        CROSS_UP: (r == 0) | (r == rows - 2), CROSS_DOWN: (r == 1) | (r == rows - 1),
     }
+
+    last_chunk = len(chunks) - 1
+    early = chunks[last_chunk][0]
+    inner = (r > 0) & (r < rows - 1)
+    to_end = {UP: r == rows - 2, DOWN: r == 1}
 
     def fetch(i):
         part = pl.ds(i * FETCH, FETCH)
@@ -90,10 +96,11 @@
             pl.when(exists[way])(f)
 
     barrier = pltpu.get_barrier_semaphore()
-    for way in range(6):
+    for way in range(8):
         guarded(way, lambda way=way: pl.semaphore_signal(
             barrier, inc=1, device_id=device[way], device_id_type=pl.DeviceIdType.MESH))
-    ends = sum(exists[way].astype(jnp.int32) for way in (UP, DOWN, RIGHT, LEFT))
+    ends = sum(exists[way].astype(jnp.int32)
+               for way in (UP, DOWN, RIGHT, LEFT, CROSS_UP, CROSS_DOWN))
 
     def remote(way, src, dst, send_sem, recv_sem):
         return pltpu.make_async_remote_copy(
@@ -151,37 +158,101 @@
         for c in range(chips):
             slot_bytes(SIBLING, 2 * c + 1 - q % 2).wait_recv()
 
-    def hop_copy(way, slot, c, src, dst):
-        return remote(way, src, dst, hop_send.at[way, slot],
-                      hop_recv.at[slot - (1 if way == DOWN else 0), c])
-
-    def send_own(c, g=None):
+    def hop_copy(way, slot, c, src, dst, sem):
+        return remote(way, src, dst, sem, hop_recv.at[slot - (1 if way == DOWN else 0), c])
+
+    def start_hop(way, c, copy, wait=False):
+        goes = exists[way]
+        if c == last_chunk:
+            goes = goes & jnp.logical_not(to_end[way])
+        pl.when(goes)(copy.wait_send if wait else copy.start)
+
+    def send_own(c, g, to_ends):
         k, n = chunks[c]
         for way in (UP, DOWN):
+            goes = to_end[way] if to_ends else exists[way] & jnp.logical_not(to_end[way])
             if g is None:
-                copy = hop_copy(way, r, c, own.at[:, pl.ds(k, n)], col[c].at[r])
+                copy = hop_copy(way, r, c, own.at[:, pl.ds(k, n)], col[c].at[r], hop_send.at[way])
             else:
-                copy = hop_copy(way, r, c, own.at[g, pl.ds(k, n)], col[c].at[r, g])
-            start(way, copy)
+                copy = hop_copy(way, r, c, own.at[g, pl.ds(k, n)], col[c].at[r, g],
+                                hop_send.at[way])
+            pl.when(goes)(copy.start)
+
+    def relay(h, way, slot, c):
+        return hop_copy(way, slot, c, col[c].at[slot], col[c].at[slot],
+                        relay_send.at[way, h - 1, c % WINDOW])
+
+    def ways(h):
+        return (r - h >= 0, r - h, UP), (r + h < rows, r + h, DOWN)
 
     def hop(h, c):
-        for cond, slot, way in ((r - h >= 0, r - h, UP), (r + h < rows, r + h, DOWN)):
+        for cond, slot, way in ways(h):
             def go(slot=slot, way=way):
-                copy = hop_copy(way, slot, c, col[c].at[slot], col[c].at[slot])
-                copy.wait_recv()
-                start(way, copy)
-
-            pl.when(cond)(go)
+                relay(h, way, slot, c).wait_recv()
+                if c >= WINDOW:
+                    start_hop(way, c, relay(h, way, slot, c - WINDOW), True)
+                start_hop(way, c, relay(h, way, slot, c))
+
+            pl.when(cond & inner if c == last_chunk else cond)(go)
+
+    def relays_sent(to_ends):
+        for h in range(1, rows):
+            for cond, slot, way in ways(h):
+                goes = to_end[way] if to_ends else exists[way] & jnp.logical_not(to_end[way])
+                top = last_chunk if to_ends else len(chunks)
+                for c in range(max(top - WINDOW, 0), top):
+                    pl.when(cond & goes)(relay(h, way, slot, c).wait_send)
 
     def hops_done():
-        for slot_cond, slot, way in [(r >= 0, r, UP), (r >= 0, r, DOWN)] + [
-                item for h in range(1, rows)
-                for item in ((r - h >= 0, r - h, UP), (r + h < rows, r + h, DOWN))]:
-            def done(slot=slot, way=way):
-                guarded(way, remote(way, own, own, hop_send.at[way, slot],
-                                    hop_send.at[way, slot]).wait_send)
-
-            pl.when(slot_cond)(done)
+        relays_sent(False)
+        for way in (UP, DOWN):
+            for end, part in ((False, own), (True, own.at[:, pl.ds(0, early)])):
+                goes = to_end[way] if end else exists[way] & jnp.logical_not(to_end[way])
+                pl.when(goes)(remote(way, part, part, hop_send.at[way], hop_send.at[way]).wait_send)
+
+    sides = ((0, r == 1, r == 0, UP, DOWN, CROSS_DOWN),
+             (1, r == rows - 2, r == rows - 1, DOWN, UP, CROSS_UP))
+
+    def pair_copy(side, way):
+        return remote(way, pairs_hbm, end_arrived.at[side], pair_sem.at[0], pair_sem.at[1 + side])
+
+    def send_pairs():
+        for side, _, end, way, _, _ in sides:
+            pl.when(end)(pair_copy(side, way).start)
+
+    def take_pairs():
+        for side, serves, end, way, _, _ in sides:
+            def take(side=side, way=way):
+                pair_copy(side, way).wait_recv()
+                keep = pltpu.make_async_copy(end_arrived.at[side], end_pairs.at[side], pair_sem.at[3])
+                keep.start()
+                keep.wait()
+
+            pl.when(end)(pair_copy(side, way).wait_send)
+            pl.when(serves)(take)
+
+    def end_copy(side, far, way):
+        return remote(way, end_stage.at[side, far],
+                      col_pick.at[:, pl.ds(far * groups, groups), pl.ds(early, bins - early)],
+                      end_send.at[side, far], end_recv.at[far])
+
+    def serve_ends():
+        for side, serves, _, _, near, cross_way in sides:
+            def serve(side=side, near=near, cross_way=cross_way):
+                for far, half, way in ((1, other, cross_way), (0, w, near)):
+                    for t in range(owned):
+                        j = end_pairs[side, 0, 0, 1, half * owned + t]
+                        end_stage[side, far, t] = col[last_chunk][j]
+                    end_copy(side, far, way).start()
+
+            pl.when(serves)(serve)
+
+    def ends_done():
+        for side, serves, end, _, near, cross_way in sides:
+            for far, way in ((1, cross_way), (0, near)):
+                copy = end_copy(side, far, way)
+                pl.when(serves)(copy.wait_send)
+                pl.when(end)(copy.wait_recv)
 
     def pick_copy(part):
         return remote(PARTNER, stage.at[1, :, :, part], col_pick.at[:, pl.ds(groups, groups), part],
@@ -192,6 +263,14 @@
             stage.at[0, :, :, part], col_pick.at[:, pl.ds(0, groups), part], pick_sem.at[2])
 
     def pick(c):
+        if c == last_chunk:
+            relays_sent(True)
+            serve_ends()
+            pl.when(inner)(lambda: pick_chunk(c))
+        else:
+            pick_chunk(c)
+
+    def pick_chunk(c):
         k, n = chunks[c]
         for side, half in ((1, other), (0, w)):
             for t in range(owned):
@@ -202,7 +281,7 @@
     for scalar in scalars:
         scalar.wait()
     fill_table(bin_ref, kcol, table, rec.shape[2])
-    split = min(AHEAD, len(chunks))
+    ahead, both = min(AHEAD, last_chunk), min(BOTH, last_chunk)
     for g in range(groups):
         for i in range(g * GROUP // FETCH, (g + 1) * GROUP // FETCH):
             fetch(i).wait()
@@ -223,15 +302,15 @@
                 col[c][r, g, :, :, lane * 128:(lane + 1) * 128] = part[k:k + n]
         if g == 0:
             pl.semaphore_wait(barrier, 2 + ends)
-        send_own(0, g)
+            send_pairs()
+        for c in range(2):
+            send_own(c, g, False)
+            send_own(c, g, True)
         to_partner(g).start()
         for way in (RIGHT, LEFT, SIBLING):
             start(way, row_copy(way, own.at[g], q, g))
-        if g == 0:
-            for c in range(1, split):
-                send_own(c, g)
-        elif split > 1:
-            send_own(1, g)
+        for c in range(2, ahead if g == 0 else both):
+            send_own(c, g, True)
     keep = pltpu.make_async_copy(own, row_set.at[q, pl.ds(0, groups)], local_sem.at[0])
     keep.start()
 
@@ -242,25 +321,33 @@
         row_work[3 + 2 * g] = lambda g=g: along_x(g)
         row_work[3 + 2 * groups + g] = lambda g=g: along_x(groups + g)
     for step in range(max(last, 3 + 3 * groups)):
-        if 2 + step < len(chunks):
-            if 2 + step < split:
-                for g in range(1, groups):
-                    send_own(2 + step, g)
-            else:
-                send_own(2 + step)
+        c = 2 + step
+        if c < len(chunks):
+            send_own(c, None, False)
+        if both <= c < ahead:
+            for g in range(1, groups):
+                send_own(c, g, True)
+        elif ahead <= c < last_chunk:
+            send_own(c, None, True)
         for h in range(1, rows):
             if 0 <= step - h + 1 < len(chunks):
                 hop(h, step - h + 1)
         if 0 <= step - rows + 2 < len(chunks):
             pick(step - rows + 2)
+        if step == 1:
+            take_pairs()
         if step in row_work:
             row_work[step]()
 
-    every = pl.ds(0, bins)
     rows_done()
     hops_done()
-    pick_copy(every).wait()
-    pick_keep(every).wait()
+    for n, goes in ((bins, inner), (early, jnp.logical_not(inner))):
+        def picks_done(n=n):
+            pick_copy(pl.ds(0, n)).wait()
+            pick_keep(pl.ds(0, n)).wait()
+
+        pl.when(goes)(picks_done)
+    ends_done()
     keep.wait()
 
 
@@ -290,6 +377,9 @@
             pltpu.VMEM((channels // 128, 2 * bins * GROUP, 128), jnp.float32),
             pltpu.VMEM((groups, bins) + tile, jnp.bfloat16),
             pltpu.VMEM((2, owned, groups, bins) + tile, jnp.bfloat16),
+            pltpu.VMEM((2, 2, owned, groups, chunks[-1][1]) + tile, jnp.bfloat16),
+            pltpu.VMEM((2,) + pairs.shape, jnp.int32),
+            pltpu.SMEM((2,) + pairs.shape, jnp.int32),
             *[pltpu.VMEM((rows, groups, n) + tile, jnp.bfloat16) for _, n in chunks],
             dma((windows // FETCH,)),
             dma((1,)),
@@ -297,9 +387,13 @@
             dma((3, cols)),
             dma((cols // 2, 2 * groups)),
             dma((cols // 2,)),
-            dma((2, rows)),
+            dma((2,)),
+            dma((2, rows - 1, WINDOW)),
             dma((rows - 1, count)),
             dma((3,)),
+            dma((4,)),
+            dma((2, 2)),
+            dma((2,)),
         ],
         compiler_params=pltpu.CompilerParams(
             collective_id=0, has_side_effects=True, vmem_limit_bytes=40 * 2**20),

time: 58.2 us -> 56.7 us (0.974)
  Pallas kernels: 56 us -> 54.6 us
    pallas_call x1, Pallas kernels: 48.1 us -> 46.7 us  [gather(): pl.pallas_call(functools.partial(gather_kernel, rows, cols, chunks), out_...]
where the time goes in v3:
time: 56.7 us; the launch traced here: 56.6 us
  Pallas kernels  54.6 us (96%)
  local copies, waits for them, and re-layouts  1.33 us (2%)
  between operations  0.67 us (1%)
    pallas_call x1, Pallas kernels, gather(): pl.pallas_call(functools.partial(gather_kernel, rows, cols, chunks), out_...  46.7 us
    pallas_call x1, Pallas kernels, cross(): pl.pallas_call(functools.partial(cross_kernel, owned), out_shape=jax.Shap...  7.89 us
    unnamed x4, local copies, waits for them, and re-layouts  1.33 us

profile of v3, /device:TPU:0, one launch (start us, length us, event | category | flops | bytes accessed | tf_op | source)
XLA Modules:
  0.0 56.6 jit_solution(13488204053278317660)
XLA Ops:
  0.7 0.0 copy-start
  0.7 0.7 %copy-done = s32[1,1,4,2]{2,3,1,0:T(2,128)S(1)} copy-done((s32[1,1,4,2]{2,3,1,0:T(2,128)S(1)}, s32[1,1,4,2]{2,3,1,0:T(2,128)}, u32[]{:S(2)}) %copy-start) | copy-done | bytes 56
  1.3 0.0 copy-start.1
  1.3 0.7 %copy-done.1 = s32[32]{0:T(128)S(1)} copy-done((s32[32]{0:T(128)S(1)}, s32[32]{0:T(128)}, u32[]{:S(2)}) %copy-start.1) | copy-done | bytes 152
  2.0 46.7 %shard_map.46 = (bf16[4,4,32,16,256]{4,3,2,1,0:T(8,128)(2,1)S(1)}, bf16[2,4,32,16,256]{4,3,2,1,0:T(8,128)(2,1)S(1)}) custom-call(s32[1,1,2,4]{3,2,1,0:T(2,128)S(1)} %bitcast.4, s32[32]{0:T(128)S(1)} %copy-done.1, bf16[16,256,1024]{2,1,0:T(8,128)(2,1)} %rec_hbm.1), custom_call_target="tpu_custom_call" | custom-call | flops 536870912 | bytes 8388608 | tf_op jit(solution)/shard_map/pallas_call | solution.py:363
  48.7 7.9 %shard_map.47 = bf16[1,1,2,2,32,256,256]{6,5,4,3,2,1,0:T(8,128)(2,1)} custom-call(s32[1,1,2,4]{3,2,1,0:T(2,128)S(1)} %bitcast.5, s32[1]{0:T(128)} %bitcast.3.count, s32[1]{0:T(128)} %bitcast.2.place, bf16[4,4,32,16,256]{4,3,2,1,0:T(8,128)(2,1)S(1)} %get-tuple-element.7.row_set, bf16[2,4,32,16,256]{4,3,2,1,0:T(8,128)(2,1)S(1)} %get-tuple-element.8.col_pick), custom_call_target="tpu_custom_call" | custom-call | flops 1073741824 | bytes 16777216 | tf_op jit(solution)/shard_map/pallas_call | solution.py:459
Async XLA Ops:
  0.7 0.7 %copy-start = (s32[1,1,4,2]{2,3,1,0:T(2,128)S(1)}, s32[1,1,4,2]{2,3,1,0:T(2,128)}, u32[]{:S(2)}) copy-start(s32[1,1,4,2]{2,3,1,0:T(2,128)} %param.5) | copy-start | bytes 100
  1.3 0.7 %copy-start.1 = (s32[32]{0:T(128)S(1)}, s32[32]{0:T(128)}, u32[]{:S(2)}) copy-start(s32[32]{0:T(128)} %bin_hbm.1) | copy-start | bytes 388

commit v4 on v3

--- a/solution.py
+++ b/solution.py
@@ -18,7 +18,10 @@
 
 def chunk_list(bins):
     size = max(bins // 8, 1)
-    return [(k, min(size, bins - k)) for k in range(0, bins, size)]
+    starts = list(range(0, 6 * size, size))
+    if size > 3:
+        starts += [6 * size - size // 2, 6 * size + size // 4]
+    return [(a, b - a) for a, b in zip(starts, starts[1:] + [bins])]
 
 
 def cos_sin(phase, length):
@@ -35,11 +38,11 @@
     return cosine, sine
 
 
-def fill_table(bin_ref, kcol, table, length):
+def fill_table(facts, kcol, table, length):
     assert length & (length - 1) == 0
     bins = kcol.shape[0]
     for k in range(bins):
-        kcol[k:k + 1, :] = jnp.full((1, 128), bin_ref[k], jnp.int32)
+        kcol[k:k + 1, :] = jnp.full((1, 128), facts[2, k], jnp.int32)
     for lane in range(0, length, 128):
         samples = lax.broadcasted_iota(jnp.int32, (8, 128), 1) + lane
         taper = 0.5 - 0.5 * cos_sin(samples, length)[0]
@@ -50,8 +53,8 @@
         table[bins:, lane:lane + 128] = (-taper * sine).astype(jnp.bfloat16)
 
 
-def gather_kernel(rows, cols, chunks, pairs_hbm, bin_hbm, rec_hbm, row_set, col_pick,
-                  pairs, bin_ref, scalar_sem, kcol, table, rec, spec, own, stage,
+def gather_kernel(rows, cols, chunks, facts_hbm, rec_hbm, row_set, col_pick,
+                  facts, facts_sem, kcol, table, rec, spec, own, stage,
                   end_stage, end_arrived, end_pairs, *rest):
     col = rest[:len(chunks)]
     (rec_sem, local_sem, partner_send, row_send, row_recv, sibling_recv, hop_send, relay_send, hop_recv,
@@ -82,10 +85,8 @@
         part = pl.ds(i * FETCH, FETCH)
         return pltpu.make_async_copy(rec_hbm.at[part], rec.at[part], rec_sem.at[i])
 
-    scalars = [pltpu.make_async_copy(bin_hbm, bin_ref, scalar_sem.at[0]),
-               pltpu.make_async_copy(pairs_hbm, pairs, scalar_sem.at[1])]
-    for scalar in scalars:
-        scalar.start()
+    get_facts = pltpu.make_async_copy(facts_hbm, facts, facts_sem.at[0])
+    get_facts.start()
     for i in range(groups * GROUP // FETCH):
         fetch(i).start()
 
@@ -214,7 +215,7 @@
              (1, r == rows - 2, r == rows - 1, DOWN, UP, CROSS_UP))
 
     def pair_copy(side, way):
-        return remote(way, pairs_hbm, end_arrived.at[side], pair_sem.at[0], pair_sem.at[1 + side])
+        return remote(way, facts_hbm, end_arrived.at[side], pair_sem.at[0], pair_sem.at[1 + side])
 
     def send_pairs():
         for side, _, end, way, _, _ in sides:
@@ -241,7 +242,7 @@
             def serve(side=side, near=near, cross_way=cross_way):
                 for far, half, way in ((1, other, cross_way), (0, w, near)):
                     for t in range(owned):
-                        j = end_pairs[side, 0, 0, 1, half * owned + t]
+                        j = end_pairs[side, 1, half * owned + t]
                         end_stage[side, far, t] = col[last_chunk][j]
                     end_copy(side, far, way).start()
 
@@ -274,13 +275,12 @@
         k, n = chunks[c]
         for side, half in ((1, other), (0, w)):
             for t in range(owned):
-                j = pairs[0, 0, 1, half * owned + t]
+                j = facts[1, half * owned + t]
                 stage[side, t, :, k:k + n] = col[c][j]
             (pick_copy if side else pick_keep)(pl.ds(k, n)).start()
 
-    for scalar in scalars:
-        scalar.wait()
-    fill_table(bin_ref, kcol, table, rec.shape[2])
+    get_facts.wait()
+    fill_table(facts, kcol, table, rec.shape[2])
     ahead, both = min(AHEAD, last_chunk), min(BOTH, last_chunk)
     for g in range(groups):
         for i in range(g * GROUP // FETCH, (g + 1) * GROUP // FETCH):
@@ -351,10 +351,9 @@
     keep.wait()
 
 
-def gather(records, pairs, bin_index, rows, cols, owned):
+def gather(records, facts, bins, rows, cols, owned):
     windows, channels, length = records.shape
     groups = windows // GROUP
-    bins = bin_index.shape[0]
     chunks = chunk_list(bins)
     count = len(chunks)
     hbm = pl.BlockSpec(memory_space=pl.ANY)
@@ -365,12 +364,11 @@
         out_shape=(
             jax.ShapeDtypeStruct((cols, 2 * groups, bins) + tile, jnp.bfloat16),
             jax.ShapeDtypeStruct((owned, 2 * groups, bins) + tile, jnp.bfloat16)),
-        in_specs=[pl.BlockSpec(memory_space=pltpu.HBM)] * 2 + [hbm],
+        in_specs=[hbm, hbm],
         out_specs=(hbm, hbm),
         scratch_shapes=[
-            pltpu.SMEM(pairs.shape, jnp.int32),
-            pltpu.SMEM((bins,), jnp.int32),
-            dma((2,)),
+            pltpu.SMEM(facts.shape, jnp.int32),
+            dma((1,)),
             pltpu.VMEM((bins, 128), jnp.int32),
             pltpu.VMEM((2 * bins, length), jnp.bfloat16),
             pltpu.VMEM(records.shape, jnp.bfloat16),
@@ -378,8 +376,8 @@
             pltpu.VMEM((groups, bins) + tile, jnp.bfloat16),
             pltpu.VMEM((2, owned, groups, bins) + tile, jnp.bfloat16),
             pltpu.VMEM((2, 2, owned, groups, chunks[-1][1]) + tile, jnp.bfloat16),
-            pltpu.VMEM((2,) + pairs.shape, jnp.int32),
-            pltpu.SMEM((2,) + pairs.shape, jnp.int32),
+            pltpu.VMEM((2,) + facts.shape, jnp.int32),
+            pltpu.SMEM((2,) + facts.shape, jnp.int32),
             *[pltpu.VMEM((rows, groups, n) + tile, jnp.bfloat16) for _, n in chunks],
             dma((windows // FETCH,)),
             dma((1,)),
@@ -400,10 +398,10 @@
         cost_estimate=pl.CostEstimate(
             flops=4 * windows * channels * length * bins,
             bytes_accessed=windows * channels * length * 2, transcendentals=0),
-    )(pairs, bin_index, records)
-
-
-def cross_kernel(owned, pairs, count, place, row_set, col_pick, out, ring, sem):
+    )(facts, records)
+
+
+def cross_kernel(owned, facts, row_set, col_pick, out, ring, sem):
     depth, _, step, channels, _ = ring.shape
     groups = row_set.shape[1]
     chunks = out.shape[4] // step
@@ -415,9 +413,9 @@
 
     def one(n, _):
         slot = n % depth
-        position = place[0] * owned + n // chunks
-        i = pairs[0, 0, 0, position]
-        live = position < count[0]
+        position = lax.axis_index("win") * owned + n // chunks
+        i = facts[0, position]
+        live = position < facts[3, 0]
 
         @pl.when(n >= depth)
         def _():
@@ -451,7 +449,7 @@
         copy(n).wait()
 
 
-def cross(row_set, col_pick, pairs, count, place):
+def cross(row_set, col_pick, facts):
     owned, groups, bins, entries, channels = col_pick.shape
     step = math.gcd(bins, 8)
     smem = pl.BlockSpec(memory_space=pltpu.SMEM)
@@ -460,7 +458,7 @@
         functools.partial(cross_kernel, owned),
         out_shape=jax.ShapeDtypeStruct(
             (1, 1, owned, 2, bins, channels, channels), jnp.bfloat16),
-        in_specs=[smem, smem, smem, vmem, vmem],
+        in_specs=[smem, vmem, vmem],
         out_specs=pl.BlockSpec(memory_space=pl.ANY),
         scratch_shapes=[
             pltpu.VMEM((4, 2, step, channels, channels), jnp.bfloat16),
@@ -470,16 +468,18 @@
         cost_estimate=pl.CostEstimate(
             flops=4 * owned * bins * channels * channels * groups * entries,
             bytes_accessed=4 * owned * bins * channels * channels, transcendentals=0),
-    )(pairs, count, place, row_set, col_pick)
+    )(facts, row_set, col_pick)
 
 
 def body(records, tile_pairs, tile_count, bin_index):
     rows, cols = lax.axis_size("row"), lax.axis_size("col")
     owned = tile_pairs.shape[2] // lax.axis_size("win")
-    pairs = jnp.swapaxes(tile_pairs, 2, 3)
-    row_set, col_pick = gather(records, pairs, bin_index, rows, cols, owned)
-    place = lax.axis_index("win").astype(jnp.int32).reshape(1)
-    return cross(row_set, col_pick, pairs, tile_count.reshape(-1), place)
+    slots, bins = tile_pairs.shape[2], bin_index.shape[0]
+    facts = (jnp.pad(jnp.swapaxes(tile_pairs, 2, 3).reshape(2, slots), ((0, 2), (0, 128 - slots)))
+             + jnp.pad(bin_index.reshape(1, bins), ((2, 1), (0, 128 - bins)))
+             + jnp.pad(tile_count.reshape(1, 1), ((3, 0), (0, 127))))
+    row_set, col_pick = gather(records, facts, bins, rows, cols, owned)
+    return cross(row_set, col_pick, facts)
 
 
 def solution(mesh):

time: 56.7 us -> 54.7 us (0.965)
  Pallas kernels: 54.6 us -> 53.2 us
  local copies, waits for them, and re-layouts: 1.33 us -> 0 us
  other arithmetic: 0 us -> 0.71 us
    pallas_call x1, Pallas kernels: 46.7 us -> 45.2 us  [gather(): pl.pallas_call(functools.partial(gather_kernel, rows, cols, chunks), out_...]
    unnamed x4 -> x0, local copies, waits for them, and re-layouts: 1.33 us -> none
    add x0 -> x1, other arithmetic: none -> 0.71 us  [body(): jnp.pad(jnp.swapaxes(tile_pairs, 2, 3).reshape(2, slots), ((0, 2), (0, 12...]
where the time goes in v4:
time: 54.7 us; the launch traced here: 54.5 us
  Pallas kernels  53.2 us (97%)
  other arithmetic  0.71 us (1%)
  between operations  0.66 us (1%)
    pallas_call x1, Pallas kernels, gather(): pl.pallas_call(functools.partial(gather_kernel, rows, cols, chunks), out_...  45.2 us
    pallas_call x1, Pallas kernels, cross(): pl.pallas_call(functools.partial(cross_kernel, owned), out_shape=jax.Shap...  7.95 us

profile of v4, /device:TPU:0, one launch (start us, length us, event | category | flops | bytes accessed | tf_op | source)
XLA Modules:
  0.0 54.5 jit_solution(4524308710902974119)
XLA Ops:
  0.7 0.7 %pad_add_fusion.facts_hbm.facts = s32[4,128]{1,0:T(4,128)S(1)} fusion(s32[1,1]{1,0:T(1,128)S(6)} %copy.5, s32[1,32]{1,0:T(1,128)} %bitcast.5, s32[2,4]{1,0:T(2,128)} %bitcast.4), kind=kLoop, calls=%fused_computation | loop fusion | flops 1024 | bytes 2212 | tf_op jit(solution)/shard_map/add | solution.py:478
  1.4 45.2 %shard_map.46 = (bf16[4,4,32,16,256]{4,3,2,1,0:T(8,128)(2,1)S(1)}, bf16[2,4,32,16,256]{4,3,2,1,0:T(8,128)(2,1)S(1)}) custom-call(s32[4,128]{1,0:T(4,128)S(1)} %pad_add_fusion.facts_hbm.facts, bf16[16,256,1024]{2,1,0:T(8,128)(2,1)} %rec_hbm.1), custom_call_target="tpu_custom_call" | custom-call | flops 536870912 | bytes 8388608 | tf_op jit(solution)/shard_map/pallas_call | solution.py:362
  46.6 7.9 %shard_map.47 = bf16[1,1,2,2,32,256,256]{6,5,4,3,2,1,0:T(8,128)(2,1)} custom-call(s32[4,128]{1,0:T(4,128)S(1)} %pad_add_fusion.facts_hbm.facts, bf16[4,4,32,16,256]{4,3,2,1,0:T(8,128)(2,1)S(1)} %get-tuple-element.7.row_set, bf16[2,4,32,16,256]{4,3,2,1,0:T(8,128)(2,1)S(1)} %get-tuple-element.8.col_pick), custom_call_target="tpu_custom_call" | custom-call | flops 1073741824 | bytes 16777216 | tf_op jit(solution)/shard_map/pallas_call | solution.py:457

commit v5 on v4

--- a/solution.py
+++ b/solution.py
@@ -405,11 +405,15 @@
     depth, _, step, channels, _ = ring.shape
     groups = row_set.shape[1]
     chunks = out.shape[4] // step
-
-    def copy(n):
-        part = pl.ds((n % chunks) * step, step)
+    piece = step // sem.shape[1]
+
+    def copy(n, p):
         return pltpu.make_async_copy(
-            ring.at[n % depth], out.at[0, 0, n // chunks, :, part], sem.at[n % depth])
+            ring.at[n % depth, :, pl.ds(p * piece, piece)],
+            out.at[0, 0, n // chunks, :, pl.ds((n % chunks) * step + p * piece, piece)],
+            sem.at[n % depth, p])
+
+    pieces = range(sem.shape[1])
 
     def one(n, _):
         slot = n % depth
@@ -419,39 +423,45 @@
 
         @pl.when(n >= depth)
         def _():
-            copy(n - depth).wait()
+            for p in pieces:
+                copy(n - depth, p).wait()
 
         @pl.when(live)
         def _():
-            for t in range(step):
-                k = (n % chunks) * step + t
-                a = row_set[i, :, k].reshape(-1, channels)
-                b = col_pick[n // chunks, :, k].reshape(a.shape)
-                parts = b.astype(jnp.float32).reshape(groups, 2, GROUP, channels)
-                turned = jnp.concatenate([-parts[:, 1:], parts[:, :1]], axis=1)
-                turned = turned.reshape(a.shape).astype(jnp.bfloat16)
-                both = lax.dot_general(
-                    a, jnp.concatenate([b, turned], axis=1), (((0,), (0,)), ((), ())),
-                    preferred_element_type=jnp.float32)
-                ring[slot, 0, t] = both[:, :channels].astype(jnp.bfloat16)
-                ring[slot, 1, t] = both[:, channels:].astype(jnp.bfloat16)
+            for p in pieces:
+                for t in range(p * piece, (p + 1) * piece):
+                    k = (n % chunks) * step + t
+                    a = row_set[i, :, k].reshape(-1, channels)
+                    b = col_pick[n // chunks, :, k].reshape(a.shape)
+                    parts = b.astype(jnp.float32).reshape(groups, 2, GROUP, channels)
+                    turned = jnp.concatenate([-parts[:, 1:], parts[:, :1]], axis=1)
+                    turned = turned.reshape(a.shape).astype(jnp.bfloat16)
+                    both = lax.dot_general(
+                        a, jnp.concatenate([b, turned], axis=1), (((0,), (0,)), ((), ())),
+                        preferred_element_type=jnp.float32)
+                    ring[slot, 0, t] = both[:, :channels].astype(jnp.bfloat16)
+                    ring[slot, 1, t] = both[:, channels:].astype(jnp.bfloat16)
+                copy(n, p).start()
 
         @pl.when(jnp.logical_not(live))
         def _():
             ring[slot] = jnp.zeros(ring.shape[1:], jnp.bfloat16)
-
-        copy(n).start()
+            for p in pieces:
+                copy(n, p).start()
+
         return 0
 
     total = owned * chunks
     lax.fori_loop(0, total, one, 0)
     for n in range(max(total - depth, 0), total):
-        copy(n).wait()
+        for p in pieces:
+            copy(n, p).wait()
 
 
 def cross(row_set, col_pick, facts):
     owned, groups, bins, entries, channels = col_pick.shape
-    step = math.gcd(bins, 8)
+    step = math.gcd(bins, 16)
+    piece = math.gcd(step, 4)
     smem = pl.BlockSpec(memory_space=pltpu.SMEM)
     vmem = pl.BlockSpec(memory_space=pltpu.VMEM)
     return pl.pallas_call(
@@ -461,8 +471,8 @@
         in_specs=[smem, vmem, vmem],
         out_specs=pl.BlockSpec(memory_space=pl.ANY),
         scratch_shapes=[
-            pltpu.VMEM((4, 2, step, channels, channels), jnp.bfloat16),
-            pltpu.SemaphoreType.DMA((4,)),
+            pltpu.VMEM((2, 2, step, channels, channels), jnp.bfloat16),
+            pltpu.SemaphoreType.DMA((2, step // piece)),
         ],
         compiler_params=pltpu.CompilerParams(vmem_limit_bytes=40 * 2**20),
         cost_estimate=pl.CostEstimate(

time: 54.7 us -> 53.7 us (0.982)
  Pallas kernels: 53.2 us -> 52.1 us
    pallas_call x1, Pallas kernels: 7.95 us -> 6.93 us  [cross(): pl.pallas_call(functools.partial(cross_kernel, owned), out_shape=jax.Shap...]
where the time goes in v5:
time: 53.7 us; the launch traced here: 53.5 us
  Pallas kernels  52.1 us (97%)
  other arithmetic  0.71 us (1%)
  between operations  0.66 us (1%)
    pallas_call x1, Pallas kernels, gather(): pl.pallas_call(functools.partial(gather_kernel, rows, cols, chunks), out_...  45.2 us
    pallas_call x1, Pallas kernels, cross(): pl.pallas_call(functools.partial(cross_kernel, owned), out_shape=jax.Shap...  6.93 us

profile of v5, /device:TPU:0, one launch (start us, length us, event | category | flops | bytes accessed | tf_op | source)
XLA Modules:
  0.0 53.5 jit_solution(11189610345257429353)
XLA Ops:
  0.7 0.7 %pad_add_fusion.facts_hbm.facts = s32[4,128]{1,0:T(4,128)S(1)} fusion(s32[1,1]{1,0:T(1,128)S(6)} %copy.5, s32[1,32]{1,0:T(1,128)} %bitcast.5, s32[2,4]{1,0:T(2,128)} %bitcast.4), kind=kLoop, calls=%fused_computation | loop fusion | flops 1024 | bytes 2212 | tf_op jit(solution)/shard_map/add | solution.py:488
  1.4 45.2 %shard_map.46 = (bf16[4,4,32,16,256]{4,3,2,1,0:T(8,128)(2,1)S(1)}, bf16[2,4,32,16,256]{4,3,2,1,0:T(8,128)(2,1)S(1)}) custom-call(s32[4,128]{1,0:T(4,128)S(1)} %pad_add_fusion.facts_hbm.facts, bf16[16,256,1024]{2,1,0:T(8,128)(2,1)} %rec_hbm.1), custom_call_target="tpu_custom_call" | custom-call | flops 536870912 | bytes 8388608 | tf_op jit(solution)/shard_map/pallas_call | solution.py:362
  46.6 6.9 %shard_map.47 = bf16[1,1,2,2,32,256,256]{6,5,4,3,2,1,0:T(8,128)(2,1)} custom-call(s32[4,128]{1,0:T(4,128)S(1)} %pad_add_fusion.facts_hbm.facts, bf16[4,4,32,16,256]{4,3,2,1,0:T(8,128)(2,1)S(1)} %get-tuple-element.7.row_set, bf16[2,4,32,16,256]{4,3,2,1,0:T(8,128)(2,1)S(1)} %get-tuple-element.8.col_pick), custom_call_target="tpu_custom_call" | custom-call | flops 1073741824 | bytes 16777216 | tf_op jit(solution)/shard_map/pallas_call | solution.py:467

commit v6 on v5

--- a/solution.py
+++ b/solution.py
@@ -81,13 +81,18 @@
     inner = (r > 0) & (r < rows - 1)
     to_end = {UP: r == rows - 2, DOWN: r == 1}
 
+    halves = spec.shape[0]
+    pieces = [(v, lane * 128, 128) for lane in range(halves) for v in range(0, GROUP, FETCH)]
+    pieces += [(v, 0, halves * 128) for v in range(GROUP, groups * GROUP, FETCH)]
+
     def fetch(i):
-        part = pl.ds(i * FETCH, FETCH)
+        v, c, n = pieces[i]
+        part = (pl.ds(v, FETCH), pl.ds(c, n))
         return pltpu.make_async_copy(rec_hbm.at[part], rec.at[part], rec_sem.at[i])
 
     get_facts = pltpu.make_async_copy(facts_hbm, facts, facts_sem.at[0])
     get_facts.start()
-    for i in range(groups * GROUP // FETCH):
+    for i in range(len(pieces)):
         fetch(i).start()
 
     def guarded(way, f):
@@ -179,6 +184,13 @@
                                 hop_send.at[way])
             pl.when(goes)(copy.start)
 
+    def send_half(c, lane):
+        part = (0, pl.ds(*chunks[c]), slice(None), pl.ds(lane * 128, 128))
+        for way in (UP, DOWN):
+            pl.when(to_end[way])(hop_copy(
+                way, r, c, own.at[part], col[c].at[(r, 0) + (slice(None),) * 2 + part[3:]],
+                hop_send.at[way]).start)
+
     def relay(h, way, slot, c):
         return hop_copy(way, slot, c, col[c].at[slot], col[c].at[slot],
                         relay_send.at[way, h - 1, c % WINDOW])
@@ -217,7 +229,7 @@
     def pair_copy(side, way):
         return remote(way, facts_hbm, end_arrived.at[side], pair_sem.at[0], pair_sem.at[1 + side])
 
-    def send_pairs():
+    def send_facts():
         for side, _, end, way, _, _ in sides:
             pl.when(end)(pair_copy(side, way).start)
 
@@ -282,34 +294,50 @@
     get_facts.wait()
     fill_table(facts, kcol, table, rec.shape[2])
     ahead, both = min(AHEAD, last_chunk), min(BOTH, last_chunk)
+    def transform(i):
+        fetch(i).wait()
+        first, c, n = pieces[i]
+        for v in range(first, first + FETCH):
+            s = lax.dot_general(table[...], rec[v, c:c + n], (((1,), (1,)), ((), ())),
+                                preferred_element_type=jnp.float32)
+            scale = 1.0 / jnp.sqrt(jnp.mean(s * s, axis=0, keepdims=True) + 1e-06)
+            s = s * scale
+            for lane in range(c // 128, (c + n) // 128):
+                part = s[:, lane * 128 - c:(lane + 1) * 128 - c]
+                spec[lane, pl.ds(v % GROUP, bins, stride=2 * GROUP), :] = part[:bins]
+                spec[lane, pl.ds(v % GROUP + GROUP, bins, stride=2 * GROUP), :] = part[bins:]
+
+    def settle(g, lane):
+        part = spec[lane].astype(jnp.bfloat16).reshape(bins, 2 * GROUP, 128)
+        own[g, :, :, lane * 128:(lane + 1) * 128] = part
+        for c, (k, n) in enumerate(chunks):
+            col[c][r, g, :, :, lane * 128:(lane + 1) * 128] = part[k:k + n]
+
     for g in range(groups):
-        for i in range(g * GROUP // FETCH, (g + 1) * GROUP // FETCH):
-            fetch(i).wait()
-            for v in range(i * FETCH, (i + 1) * FETCH):
-                s = lax.dot_general(table[...], rec[v], (((1,), (1,)), ((), ())),
-                                    preferred_element_type=jnp.float32)
-                scale = 1.0 / jnp.sqrt(jnp.mean(s * s, axis=0, keepdims=True) + 1e-06)
-                s = s * scale
-                first = v % GROUP
-                for lane in range(spec.shape[0]):
-                    part = s[:, lane * 128:(lane + 1) * 128]
-                    spec[lane, pl.ds(first, bins, stride=2 * GROUP), :] = part[:bins]
-                    spec[lane, pl.ds(first + GROUP, bins, stride=2 * GROUP), :] = part[bins:]
-        for lane in range(spec.shape[0]):
-            part = spec[lane].astype(jnp.bfloat16).reshape(bins, 2 * GROUP, 128)
-            own[g, :, :, lane * 128:(lane + 1) * 128] = part
-            for c, (k, n) in enumerate(chunks):
-                col[c][r, g, :, :, lane * 128:(lane + 1) * 128] = part[k:k + n]
+        mine = [i for i, piece in enumerate(pieces) if piece[0] // GROUP == g]
         if g == 0:
-            pl.semaphore_wait(barrier, 2 + ends)
-            send_pairs()
+            for lane in range(halves):
+                for i in mine[lane * len(mine) // halves:(lane + 1) * len(mine) // halves]:
+                    transform(i)
+                settle(g, lane)
+                if lane == 0:
+                    pl.semaphore_wait(barrier, 2 + ends)
+                for c in range(ahead):
+                    send_half(c, lane)
+            send_facts()
+        else:
+            for i in mine:
+                transform(i)
+            for lane in range(halves):
+                settle(g, lane)
         for c in range(2):
             send_own(c, g, False)
-            send_own(c, g, True)
+            if g > 0:
+                send_own(c, g, True)
         to_partner(g).start()
         for way in (RIGHT, LEFT, SIBLING):
             start(way, row_copy(way, own.at[g], q, g))
-        for c in range(2, ahead if g == 0 else both):
+        for c in range(2, both if g > 0 else 2):
             send_own(c, g, True)
     keep = pltpu.make_async_copy(own, row_set.at[q, pl.ds(0, groups)], local_sem.at[0])
     keep.start()
@@ -379,7 +407,7 @@
             pltpu.VMEM((2,) + facts.shape, jnp.int32),
             pltpu.SMEM((2,) + facts.shape, jnp.int32),
             *[pltpu.VMEM((rows, groups, n) + tile, jnp.bfloat16) for _, n in chunks],
-            dma((windows // FETCH,)),
+            dma((windows // FETCH + (channels // 128 - 1) * GROUP // FETCH,)),
             dma((1,)),
             dma((1,)),
             dma((3, cols)),

time: 53.7 us -> 53 us (0.987)
  Pallas kernels: 52.1 us -> 51.4 us
    pallas_call x1, Pallas kernels: 45.2 us -> 44.5 us  [gather(): pl.pallas_call(functools.partial(gather_kernel, rows, cols, chunks), out_...]
where the time goes in v6:
time: 53 us; the launch traced here: 52.8 us
  Pallas kernels  51.4 us (97%)
  other arithmetic  0.71 us (1%)
  between operations  0.66 us (1%)
    pallas_call x1, Pallas kernels, gather(): pl.pallas_call(functools.partial(gather_kernel, rows, cols, chunks), out_...  44.5 us
    pallas_call x1, Pallas kernels, cross(): pl.pallas_call(functools.partial(cross_kernel, owned), out_shape=jax.Shap...  6.93 us

profile of v6, /device:TPU:0, one launch (start us, length us, event | category | flops | bytes accessed | tf_op | source)
XLA Modules:
  0.0 52.8 jit_solution(15336646590617506972)
XLA Ops:
  0.7 0.7 %pad_add_fusion.facts_hbm.facts = s32[4,128]{1,0:T(4,128)S(1)} fusion(s32[1,1]{1,0:T(1,128)S(6)} %copy.5, s32[1,32]{1,0:T(1,128)} %bitcast.5, s32[2,4]{1,0:T(2,128)} %bitcast.4), kind=kLoop, calls=%fused_computation | loop fusion | flops 1024 | bytes 2212 | tf_op jit(solution)/shard_map/add | solution.py:516
  1.4 44.5 %shard_map.46 = (bf16[4,4,32,16,256]{4,3,2,1,0:T(8,128)(2,1)S(1)}, bf16[2,4,32,16,256]{4,3,2,1,0:T(8,128)(2,1)S(1)}) custom-call(s32[4,128]{1,0:T(4,128)S(1)} %pad_add_fusion.facts_hbm.facts, bf16[16,256,1024]{2,1,0:T(8,128)(2,1)} %rec_hbm.1), custom_call_target="tpu_custom_call" | custom-call | flops 536870912 | bytes 8388608 | tf_op jit(solution)/shard_map/pallas_call | solution.py:390
  45.9 6.9 %shard_map.47 = bf16[1,1,2,2,32,256,256]{6,5,4,3,2,1,0:T(8,128)(2,1)} custom-call(s32[4,128]{1,0:T(4,128)S(1)} %pad_add_fusion.facts_hbm.facts, bf16[4,4,32,16,256]{4,3,2,1,0:T(8,128)(2,1)S(1)} %get-tuple-element.7.row_set, bf16[2,4,32,16,256]{4,3,2,1,0:T(8,128)(2,1)S(1)} %get-tuple-element.8.col_pick), custom_call_target="tpu_custom_call" | custom-call | flops 1073741824 | bytes 16777216 | tf_op jit(solution)/shard_map/pallas_call | solution.py:495

commit v7 on v6

--- a/solution.py
+++ b/solution.py
@@ -10,7 +10,7 @@
 
 GROUP = 8
 FETCH = 4
-AHEAD = 5
+AHEAD = 6
 BOTH = 3
 WINDOW = 2
 UP, DOWN, PARTNER, RIGHT, LEFT, SIBLING, CROSS_UP, CROSS_DOWN = range(8)
@@ -118,7 +118,7 @@
 
     def row_copy(way, src, slot, part):
         recv = sibling_recv.at[slot // 2] if way == SIBLING else row_recv.at[slot // 2, part]
-        return remote(way, src, row_set.at[slot, part], row_send.at[way - RIGHT, slot], recv)
+        return remote(way, src, row_set.at[slot, part], row_send.at[way - RIGHT, slot // 2], recv)
 
     def row_arrived(slot, part):
         row_copy(RIGHT, row_set.at[slot, part], slot, part).wait_recv()
@@ -149,7 +149,7 @@
     def rows_done():
         def slot_bytes(way, slot):
             return remote(way, row_set.at[slot], row_set.at[slot],
-                          row_send.at[way - RIGHT, slot], sibling_recv.at[slot // 2])
+                          row_send.at[way - RIGHT, slot // 2], sibling_recv.at[slot // 2])
 
         remote(PARTNER, own, own, partner_send.at[0], partner_send.at[0]).wait_send()
         for way in (RIGHT, LEFT, SIBLING):
@@ -193,7 +193,7 @@
 
     def relay(h, way, slot, c):
         return hop_copy(way, slot, c, col[c].at[slot], col[c].at[slot],
-                        relay_send.at[way, h - 1, c % WINDOW])
+                        relay_send.at[way, min(h, max(rows - 2, 1)) - 1, c % WINDOW])
 
     def ways(h):
         return (r - h >= 0, r - h, UP), (r + h < rows, r + h, DOWN)
@@ -410,11 +410,11 @@
             dma((windows // FETCH + (channels // 128 - 1) * GROUP // FETCH,)),
             dma((1,)),
             dma((1,)),
-            dma((3, cols)),
+            dma((3, cols // 2)),
             dma((cols // 2, 2 * groups)),
             dma((cols // 2,)),
             dma((2,)),
-            dma((2, rows - 1, WINDOW)),
+            dma((2, max(rows - 2, 1), WINDOW)),
             dma((rows - 1, count)),
             dma((3,)),
             dma((4,)),

time: 53 us -> 52.3 us (0.987)
  Pallas kernels: 51.4 us -> 50.8 us
    pallas_call x1, Pallas kernels: 44.5 us -> 43.8 us  [gather(): pl.pallas_call(functools.partial(gather_kernel, rows, cols, chunks), out_...]
where the time goes in v7:
time: 52.3 us; the launch traced here: 52.1 us
  Pallas kernels  50.8 us (97%)
  other arithmetic  0.71 us (1%)
  between operations  0.66 us (1%)
    pallas_call x1, Pallas kernels, gather(): pl.pallas_call(functools.partial(gather_kernel, rows, cols, chunks), out_...  43.8 us
    pallas_call x1, Pallas kernels, cross(): pl.pallas_call(functools.partial(cross_kernel, owned), out_shape=jax.Shap...  6.93 us

profile of v7, /device:TPU:0, one launch (start us, length us, event | category | flops | bytes accessed | tf_op | source)
XLA Modules:
  0.0 52.1 jit_solution(10604309602883526012)
XLA Ops:
  0.7 0.7 %pad_add_fusion.facts_hbm.facts = s32[4,128]{1,0:T(4,128)S(1)} fusion(s32[1,1]{1,0:T(1,128)S(6)} %copy.5, s32[1,32]{1,0:T(1,128)} %bitcast.5, s32[2,4]{1,0:T(2,128)} %bitcast.4), kind=kLoop, calls=%fused_computation | loop fusion | flops 1024 | bytes 2212 | tf_op jit(solution)/shard_map/add | solution.py:516
  1.4 43.8 %shard_map.46 = (bf16[4,4,32,16,256]{4,3,2,1,0:T(8,128)(2,1)S(1)}, bf16[2,4,32,16,256]{4,3,2,1,0:T(8,128)(2,1)S(1)}) custom-call(s32[4,128]{1,0:T(4,128)S(1)} %pad_add_fusion.facts_hbm.facts, bf16[16,256,1024]{2,1,0:T(8,128)(2,1)} %rec_hbm.1), custom_call_target="tpu_custom_call" | custom-call | flops 536870912 | bytes 8388608 | tf_op jit(solution)/shard_map/pallas_call | solution.py:390
  45.2 6.9 %shard_map.47 = bf16[1,1,2,2,32,256,256]{6,5,4,3,2,1,0:T(8,128)(2,1)} custom-call(s32[4,128]{1,0:T(4,128)S(1)} %pad_add_fusion.facts_hbm.facts, bf16[4,4,32,16,256]{4,3,2,1,0:T(8,128)(2,1)S(1)} %get-tuple-element.7.row_set, bf16[2,4,32,16,256]{4,3,2,1,0:T(8,128)(2,1)S(1)} %get-tuple-element.8.col_pick), custom_call_target="tpu_custom_call" | custom-call | flops 1073741824 | bytes 16777216 | tf_op jit(solution)/shard_map/pallas_call | solution.py:495

commit v8 on v7

--- a/solution.py
+++ b/solution.py
@@ -11,7 +11,7 @@
 GROUP = 8
 FETCH = 4
 AHEAD = 6
-BOTH = 3
+BOTH = 4
 WINDOW = 2
 UP, DOWN, PARTNER, RIGHT, LEFT, SIBLING, CROSS_UP, CROSS_DOWN = range(8)
 

time: 52.3 us -> 52.3 us (level)
  no operation moved by 1% of the time
where the time goes in v8:
time: 52.3 us; the launch traced here: 52.1 us
  Pallas kernels  50.7 us (97%)
  other arithmetic  0.71 us (1%)
  between operations  0.66 us (1%)
    pallas_call x1, Pallas kernels, gather(): pl.pallas_call(functools.partial(gather_kernel, rows, cols, chunks), out_...  43.8 us
    pallas_call x1, Pallas kernels, cross(): pl.pallas_call(functools.partial(cross_kernel, owned), out_shape=jax.Shap...  6.93 us

profile of v8, /device:TPU:0, one launch (start us, length us, event | category | flops | bytes accessed | tf_op | source)
XLA Modules:
  0.0 52.1 jit_solution(7638589636223893790)
XLA Ops:
  0.7 0.7 %pad_add_fusion.facts_hbm.facts = s32[4,128]{1,0:T(4,128)S(1)} fusion(s32[1,1]{1,0:T(1,128)S(6)} %copy.5, s32[1,32]{1,0:T(1,128)} %bitcast.5, s32[2,4]{1,0:T(2,128)} %bitcast.4), kind=kLoop, calls=%fused_computation | loop fusion | flops 1024 | bytes 2212 | tf_op jit(solution)/shard_map/add | solution.py:516
  1.4 43.8 %shard_map.46 = (bf16[4,4,32,16,256]{4,3,2,1,0:T(8,128)(2,1)S(1)}, bf16[2,4,32,16,256]{4,3,2,1,0:T(8,128)(2,1)S(1)}) custom-call(s32[4,128]{1,0:T(4,128)S(1)} %pad_add_fusion.facts_hbm.facts, bf16[16,256,1024]{2,1,0:T(8,128)(2,1)} %rec_hbm.1), custom_call_target="tpu_custom_call" | custom-call | flops 536870912 | bytes 8388608 | tf_op jit(solution)/shard_map/pallas_call | solution.py:390
  45.2 6.9 %shard_map.47 = bf16[1,1,2,2,32,256,256]{6,5,4,3,2,1,0:T(8,128)(2,1)} custom-call(s32[4,128]{1,0:T(4,128)S(1)} %pad_add_fusion.facts_hbm.facts, bf16[4,4,32,16,256]{4,3,2,1,0:T(8,128)(2,1)S(1)} %get-tuple-element.7.row_set, bf16[2,4,32,16,256]{4,3,2,1,0:T(8,128)(2,1)S(1)} %get-tuple-element.8.col_pick), custom_call_target="tpu_custom_call" | custom-call | flops 1073741824 | bytes 16777216 | tf_op jit(solution)/shard_map/pallas_call | solution.py:495
